TPU v7x, 32 devices: a whole 2x2x4 slice. The times are simulated.
32 devices in a mesh: band: 2 (over y), col: 4 (over z), row: 2 (over x), vis: 2 (over core).
Axes of the slice: x: 2, y: 2, z: 4, core: 2. Of those that a mesh axis runs over, the one named last changes fastest.
Arguments:
- visibilities: bfloat16 [3072, 2, 256], P(('band', 'col', 'row', 'vis')), parts along dimension 0, may hold values from -6 to 6
- coords: float32 [3072, 2, 256], P(('band', 'col', 'row', 'vis')), parts along dimension 0, may hold values from -0.5 to 0.5
- block_subgrid: int32 [3072], P(('band', 'col', 'row', 'vis')), parts along dimension 0, may hold values from 0 to 1023, as said below
- baseline_ids: int32 [3072], P(('band', 'col', 'row', 'vis')), parts along dimension 0, may hold values from 0 to 130815
- live_blocks: int32 [32], P(('band', 'col', 'row', 'vis')), parts along dimension 0, may hold values from 48 to 96, as said below
- subgrid_place: int32 [3, 2048], P(None, ('band', 'col', 'row', 'vis')), parts along dimension 1, may hold values from 0 to 1984, as said below
- baseline_weight: float32 [130816], replicated, may hold values from 0.2 to 2
- tapering: float32 [64, 64], replicated, may hold values from 0.2 to 1
- plane_phase: float32 [8, 64, 64], replicated, may hold values from -3.140625 to 3.140625
Outputs:
- grid: float32 [2, 4096, 1024], P(None, ('band', 'col'), ('row', 'vis')), parts along dimension 1
There are 2 independent parts, one for each index of `band`. A program takes and returns all parts, laid end to end along the dimension named above; an argument that names none is the same for every part. Nothing has to cross between parts.
Inputs may be any that keep to these rules, and one draw needn't show every extreme that they name: `block_subgrid`: subgrid s is owned by the device s // 64, devices counted in the order col, row, vis. Of the 96 blocks of one device at most 24 name subgrids of one owner, and in every draw some owner is named 24 times by the blocks of every device. `live_blocks`: blocks j of device d with j >= entry d carry no weight. Some device has all 96 blocks live and some has 48. `subgrid_place`: row 2 is a subgrid's w-plane, below 8. Every subgrid lies inside one facet: for some c and r its u cells lie in c * 512 .. (c + 1) * 512 - 1 and its v cells in r * 512 .. (r + 1) * 512 - 1. At most 16 of one owner's 64 subgrids lie in one facet, and in every draw the last facet holds 16 subgrids of every owner.
All inputs are finite; a program needn't handle non-finite values.
Results may differ from a plain program's by a relative error of at most 0.0037.
Values sent between devices are 32-bit elements; how exact they have to be, the bound alone decides.
A program may use at most 128 MiB of HBM per device.

v0:
```python
import math

import jax
import jax.numpy as jnp
from jax import lax
from jax.sharding import PartitionSpec as P

SG = 64
BV = 256
FU = 512
FV = 512


def kernel_operands(coords, weighted):
    centred = (jnp.arange(SG) - SG // 2).astype(coords.dtype)
    angle_u = 2.0 * math.pi * coords[:, 0, :, None] * centred
    vertical_angle = 2.0 * math.pi * coords[:, 1, :, None] * centred
    kern_ure = jnp.cos(angle_u)
    kern_uim = jnp.sin(angle_u)
    kernel_vertical_real = jnp.cos(vertical_angle)
    kernel_vertical_imag = jnp.sin(vertical_angle)
    vis_real = weighted[:, 0, :, None]
    vis_imag = weighted[:, 1, :, None]
    scaled_re = vis_real * kern_ure - vis_imag * kern_uim
    scaled_im = vis_real * kern_uim + vis_imag * kern_ure
    left_side = jnp.concatenate([scaled_re, scaled_im], axis=1).astype(jnp.bfloat16)
    upper_limit = jnp.concatenate([kernel_vertical_real, kernel_vertical_imag], axis=2)
    lower_limit = jnp.concatenate([-kernel_vertical_imag, kernel_vertical_real], axis=2)
    right_side = jnp.concatenate([upper_limit, lower_limit], axis=1).astype(jnp.bfloat16)
    return (left_side, right_side)


def bucket_rank(labels, buckets):
    member = (labels[:, None] == jnp.arange(buckets)[None, :]).astype(jnp.int32)
    earlier = jnp.cumsum(member, axis=0) - member
    return jnp.sum(earlier * member, axis=1)


def on_device(
    visibilities,
    coords,
    block_subgrid,
    baseline_ids,
    live_blocks,
    subgrid_place,
    baseline_weight,
    tapering,
    plane_phase,
):
    nblocks = visibilities.shape[0]
    width = visibilities.shape[2]
    n_col = lax.axis_size("col")
    n_row = lax.axis_size("row")
    n_vis = lax.axis_size("vis")
    devices = n_col * n_row * n_vis
    facets = n_col * n_row
    sub_dev = subgrid_place.shape[1]
    capacity = 4 * nblocks // devices
    sub_cap = 2 * sub_dev // facets
    slots = devices * capacity
    high = lax.Precision.HIGHEST
    live = jnp.arange(nblocks) < live_blocks[0]
    weight = jnp.where(live, jnp.take(baseline_weight, baseline_ids), 0.0)
    weighted = visibilities.astype(jnp.float32) * weight[:, None, None]
    payload = jnp.concatenate([weighted, coords], axis=1)
    owner = block_subgrid // sub_dev
    local_sub = (block_subgrid % sub_dev).astype(jnp.float32)
    target = owner * capacity + bucket_rank(owner, devices)
    send_rows = jnp.zeros((slots, 4, width), jnp.float32).at[target].set(payload)
    send_subs = jnp.zeros((slots,), jnp.float32).at[target].set(local_sub)
    got_rows, got_subs = (
        lax.all_to_all(
            send_rows.reshape(devices, capacity, 4, width),
            ("col", "row", "vis"),
            split_axis=0,
            concat_axis=0,
            tiled=True,
        ),
        lax.all_to_all(
            send_subs.reshape(devices, capacity),
            ("col", "row", "vis"),
            split_axis=0,
            concat_axis=0,
            tiled=True,
        ),
    )
    group = min(64, slots)
    slot_rows = got_rows.reshape(slots // group, group, 4, width)
    slot_subs = got_subs.reshape(slots // group, group).astype(jnp.int32)

    def grid_group(subgrid_sum, items):
        block, labels = items
        left_side, right_side = kernel_operands(block[:, 2:], block[:, :2])
        image = jnp.einsum(
            "gkx,gky->gxy", left_side, right_side, preferred_element_type=jnp.float32
        )
        member = (labels[:, None] == jnp.arange(sub_dev)[None, :]).astype(jnp.float32)
        return (subgrid_sum + jnp.einsum("gs,gxy->sxy", member, image, precision=high), None)

    start = jnp.zeros((sub_dev, SG, 2 * SG), jnp.float32)
    subgrid_sum, _ = lax.scan(grid_group, start, (slot_rows, slot_subs))
    image_re = subgrid_sum[:, :, :SG]
    image_im = subgrid_sum[:, :, SG:]
    phase = jnp.take(plane_phase, subgrid_place[2], axis=0)
    screen_re = tapering * jnp.cos(phase)
    screen_im = tapering * jnp.sin(phase)
    masked = jnp.concatenate(
        [image_re * screen_re - image_im * screen_im, image_re * screen_im + image_im * screen_re],
        axis=2,
    )
    freq = jnp.arange(SG)
    turns = (freq[:, None] * freq[None, :] % SG).astype(jnp.float32) * (2.0 * math.pi / SG)
    table_re = jnp.cos(turns)
    table_im = -jnp.sin(turns)
    first_re = jnp.einsum("kl,slc->skc", table_re, masked, precision=high)
    first_im = jnp.einsum("kl,slc->skc", table_im, masked, precision=high)
    halfway = first_re + jnp.concatenate([-first_im[:, :, SG:], first_im[:, :, :SG]], axis=2)
    second = jnp.concatenate(
        [
            jnp.concatenate([table_re, table_im], axis=1),
            jnp.concatenate([-table_im, table_re], axis=1),
        ],
        axis=0,
    )
    spectrum = jnp.einsum("skc,cd->skd", halfway, second, precision=high) * (
        1.0 / (SG * math.sqrt(BV))
    )
    corner_u = subgrid_place[0]
    corner_v = subgrid_place[1]
    facet = corner_u // FU * n_row + corner_v // FV
    facet_slot = facet * sub_cap + bucket_rank(facet, facets)
    offsets = jnp.stack([corner_u % FU, corner_v % FV], axis=1).astype(jnp.float32)
    send_grid = jnp.zeros((facets * sub_cap, SG, 2 * SG), jnp.float32).at[facet_slot].set(spectrum)
    send_offsets = jnp.zeros((facets * sub_cap, 2), jnp.float32).at[facet_slot].set(offsets)
    recv_grid, recv_offsets = (
        lax.all_to_all(
            lax.all_to_all(
                send_grid.reshape(n_col, n_row, sub_cap, SG, 2 * SG),
                "col",
                split_axis=0,
                concat_axis=0,
                tiled=True,
            ),
            "row",
            split_axis=1,
            concat_axis=1,
            tiled=True,
        ),
        lax.all_to_all(
            lax.all_to_all(
                send_offsets.reshape(n_col, n_row, sub_cap, 2),
                "col",
                split_axis=0,
                concat_axis=0,
                tiled=True,
            ),
            "row",
            split_axis=1,
            concat_axis=1,
            tiled=True,
        ),
    )
    arrived = facets * sub_cap
    recv_grid = recv_grid.reshape(arrived, SG, 2 * SG)
    recv_offsets = recv_offsets.reshape(arrived, 2).astype(jnp.int32)

    def place_one(item, partial_value):
        offset_u = recv_offsets[item, 0]
        offset_v = recv_offsets[item, 1]
        anchor = jnp.zeros((), jnp.int32)
        piece = recv_grid[item]
        both = jnp.stack([piece[:, :SG], piece[:, SG:]], axis=0)
        before = lax.dynamic_slice(partial_value, (anchor, offset_u, offset_v), (2, SG, SG))
        return lax.dynamic_update_slice(partial_value, before + both, (anchor, offset_u, offset_v))

    partial_value = lax.fori_loop(0, arrived, place_one, jnp.zeros((2, FU, FV), jnp.float32))
    return lax.psum_scatter(partial_value, "vis", scatter_dimension=2, tiled=True)


def solution(mesh):
    in_specs = (
        P(("band", "col", "row", "vis"), None, None),
        P(("band", "col", "row", "vis"), None, None),
        P(("band", "col", "row", "vis")),
        P(("band", "col", "row", "vis")),
        P(("band", "col", "row", "vis")),
        P(None, ("band", "col", "row", "vis")),
        P(),
        P(),
        P(),
    )
    out_specs = P(None, ("band", "col"), ("row", "vis"))
    return jax.shard_map(
        on_device, mesh=mesh, in_specs=in_specs, out_specs=out_specs, check_vma=False
    )
```

profile of v0, /device:TPU:31, one launch (start us, length us, event | category | flops | bytes accessed | tf_op | source)
XLA Modules:
  0.0 1730.9 jit_solution(9095762215408226787)
XLA Ops:
  9.3 6.3 all-to-all-start.2
  25.9 6.2 all-to-all-start.3
  36.5 30.9 %all-to-all-done.3 = f32[16,24,4,256]{3,1,2,0:T(8,128)} async-done(((f32[16,24,4,256]{3,1,2,0:T(8,128)}), f32[16,24,4,256]{3,1,2,0:T(8,128)}, u32[]{:S(2)}, u32[]{:S(2)}) %all-to-all-start.3) | async-done | bytes 1572896 | tf_op jit(solution)/shard_map/all_to_all | solution.py:72
  74.7 528.9 %while.27 = (s32[]{:T(128)}, f32[64,64,128]{2,0,1:T(8,128)S(1)}, s32[6,64]{1,0:T(8,128)S(1)}, f32[6,64,4,256]{3,1,0,2:T(8,128)}, s32[]{:T(128)}, /*index=5*/s32[]{:T(128)}) while((s32[]{:T(128)}, f32[64,64,128]{2,0,1:T(8,128)S(1)}, s32[6,64]{1,0:T(8,128)S(1)}, f32[6,64,4,256]{3,1,0,2:T(8,128)}, s32[]{:T(128)}, ...), condition=%wide.region_8.9_spmd.clone, body=%wide.region_7.8_spmd.clone.sunk | while | flops 997232768 | bytes 30672212 | solution.py:101
  75.8 68.3 %fusion.91 = (bf16[64,256,64]{2,1,0:T(8,128)(2,1)}, bf16[64,256,64]{2,1,0:T(8,128)(2,1)}, bf16[64,256,64]{2,1,0:T(8,128)(2,1)}, bf16[64,256,64]{2,1,0:T(8,128)(2,1)}, bf16[64,256,64]{2,1,0:T(8,128)(2,1)}) fusion(f32[64,256]{1,0:T(8,128)S(1)} %get-tuple-element.272, f32[64]{0:T(128)S(1)} %add_convert_fusion.3, f32[64,256]{1,0:T(8,128)S(1)} %get-tuple-element.273, ...), kind=kLoop, calls=%fused_computation.21.clone.1 | loop fusion | flops 14680064 | bytes 10748160 | tf_op jit(solution)/shard_map/convert.5
  144.0 13.8 fusion.92
  157.8 5.0 select_add_fusion.2
  163.9 68.3 %fusion.91 = (bf16[64,256,64]{2,1,0:T(8,128)(2,1)}, bf16[64,256,64]{2,1,0:T(8,128)(2,1)}, bf16[64,256,64]{2,1,0:T(8,128)(2,1)}, bf16[64,256,64]{2,1,0:T(8,128)(2,1)}, bf16[64,256,64]{2,1,0:T(8,128)(2,1)}) fusion(f32[64,256]{1,0:T(8,128)S(1)} %get-tuple-element.272, f32[64]{0:T(128)S(1)} %add_convert_fusion.3, f32[64,256]{1,0:T(8,128)S(1)} %get-tuple-element.273, ...), kind=kLoop, calls=%fused_computation.21.clone.1 | loop fusion | flops 14680064 | bytes 10748160 | tf_op jit(solution)/shard_map/convert.5
  232.2 13.8 fusion.92
  246.0 5.0 select_add_fusion.2
  252.1 68.3 %fusion.91 = (bf16[64,256,64]{2,1,0:T(8,128)(2,1)}, bf16[64,256,64]{2,1,0:T(8,128)(2,1)}, bf16[64,256,64]{2,1,0:T(8,128)(2,1)}, bf16[64,256,64]{2,1,0:T(8,128)(2,1)}, bf16[64,256,64]{2,1,0:T(8,128)(2,1)}) fusion(f32[64,256]{1,0:T(8,128)S(1)} %get-tuple-element.272, f32[64]{0:T(128)S(1)} %add_convert_fusion.3, f32[64,256]{1,0:T(8,128)S(1)} %get-tuple-element.273, ...), kind=kLoop, calls=%fused_computation.21.clone.1 | loop fusion | flops 14680064 | bytes 10748160 | tf_op jit(solution)/shard_map/convert.5
  320.3 13.8 fusion.92
  334.1 5.0 select_add_fusion.2
  340.2 68.3 %fusion.91 = (bf16[64,256,64]{2,1,0:T(8,128)(2,1)}, bf16[64,256,64]{2,1,0:T(8,128)(2,1)}, bf16[64,256,64]{2,1,0:T(8,128)(2,1)}, bf16[64,256,64]{2,1,0:T(8,128)(2,1)}, bf16[64,256,64]{2,1,0:T(8,128)(2,1)}) fusion(f32[64,256]{1,0:T(8,128)S(1)} %get-tuple-element.272, f32[64]{0:T(128)S(1)} %add_convert_fusion.3, f32[64,256]{1,0:T(8,128)S(1)} %get-tuple-element.273, ...), kind=kLoop, calls=%fused_computation.21.clone.1 | loop fusion | flops 14680064 | bytes 10748160 | tf_op jit(solution)/shard_map/convert.5
  408.5 13.8 fusion.92
  422.3 5.0 select_add_fusion.2
  428.4 68.3 %fusion.91 = (bf16[64,256,64]{2,1,0:T(8,128)(2,1)}, bf16[64,256,64]{2,1,0:T(8,128)(2,1)}, bf16[64,256,64]{2,1,0:T(8,128)(2,1)}, bf16[64,256,64]{2,1,0:T(8,128)(2,1)}, bf16[64,256,64]{2,1,0:T(8,128)(2,1)}) fusion(f32[64,256]{1,0:T(8,128)S(1)} %get-tuple-element.272, f32[64]{0:T(128)S(1)} %add_convert_fusion.3, f32[64,256]{1,0:T(8,128)S(1)} %get-tuple-element.273, ...), kind=kLoop, calls=%fused_computation.21.clone.1 | loop fusion | flops 14680064 | bytes 10748160 | tf_op jit(solution)/shard_map/convert.5
  496.6 13.8 fusion.92
  510.4 5.0 select_add_fusion.2
  516.5 68.3 %fusion.91 = (bf16[64,256,64]{2,1,0:T(8,128)(2,1)}, bf16[64,256,64]{2,1,0:T(8,128)(2,1)}, bf16[64,256,64]{2,1,0:T(8,128)(2,1)}, bf16[64,256,64]{2,1,0:T(8,128)(2,1)}, bf16[64,256,64]{2,1,0:T(8,128)(2,1)}) fusion(f32[64,256]{1,0:T(8,128)S(1)} %get-tuple-element.272, f32[64]{0:T(128)S(1)} %add_convert_fusion.3, f32[64,256]{1,0:T(8,128)S(1)} %get-tuple-element.273, ...), kind=kLoop, calls=%fused_computation.21.clone.1 | loop fusion | flops 14680064 | bytes 10748160 | tf_op jit(solution)/shard_map/convert.5
  584.8 13.8 fusion.92
  598.6 5.0 select_add_fusion.2
  605.2 8.8 multiply_subtract_fusion
  624.3 8.7 scatter_fusion.1
  633.0 4.9 all-to-all-start.4
  638.5 89.7 %all-to-all-done.4 = f32[4,2,16,64,128]{4,3,2,1,0:T(8,128)} async-done(((f32[4,2,16,64,128]{4,3,2,1,0:T(8,128)}), f32[4,2,16,64,128]{4,3,2,1,0:T(8,128)}, u32[]{:S(2)}, u32[]{:S(2)}) %all-to-all-start.4) | async-done | bytes 4194336 | tf_op jit(solution)/shard_map/all_to_all | solution.py:137
  731.4 4.7 copy.46
  736.1 5.6 all-to-all-start.5
  743.3 42.0 %all-to-all-done.5 = f32[4,2,16,64,128]{4,3,2,0,1:T(8,128)} async-done(((f32[4,2,16,64,128]{4,3,2,0,1:T(8,128)}), f32[4,2,16,64,128]{4,3,2,0,1:T(8,128)}, u32[]{:S(2)}, u32[]{:S(2)}) %all-to-all-start.5) | async-done | bytes 4194336 | tf_op jit(solution)/shard_map/all_to_all | solution.py:136
  785.3 4.7 copy.47
  790.2 920.4 %while.26 = (s32[]{:T(128)}, f32[2,512,512]{2,1,0:T(8,128)S(1)}, s32[128,2]{0,1:T(2,128)S(1)}, f32[128,64,128]{2,1,0:T(8,128)}, s32[]{:T(128)}, /*index=5*/s32[]{:T(128)}, s32[]{:T(128)}) while((s32[]{:T(128)}, f32[2,512,512]{2,1,0:T(8,128)S(1)}, s32[128,2]{0,1:T(2,128)S(1)}, f32[128,64,128]{2,1,0:T(8,128)}, s32[]{:T(128)}, ...), condition=%wide.region_11.12_spmd, body=%wide.region_10.11_spmd.sunk | while | flops 16392 | bytes 295093 | solution.py:176
  1712.0 12.0 reduce-scatter.2.cloned.1.call-done
  (734 shorter events, 471.3 us)
Async XLA Ops:
  6.5 10.4 copy-start
  9.3 16.7 all-to-all-start.2
  25.9 6.2 copy-start.6
  25.9 8.2 copy-start.2
  25.9 41.5 %all-to-all-start.3 = ((f32[16,24,4,256]{3,1,2,0:T(8,128)}), f32[16,24,4,256]{3,1,2,0:T(8,128)}, u32[]{:S(2)}, u32[]{:S(2)}) async-start(f32[16,24,4,256]{3,1,2,0:T(8,128)} %copy.41), calls=%async_computation.3 | async-start | bytes 3145728 | tf_op jit(solution)/shard_map/all_to_all | solution.py:72
  67.4 565.6 %all-to-all-start = ((f32[4,2,16,2]{2,3,1,0:T(2,128)}), f32[4,2,16,2]{2,3,1,0:T(2,128)S(1)}, u32[]{:S(2)}, u32[]{:S(2)}) async-start(f32[4,2,16,2]{2,3,1,0:T(2,128)} %copy.38), calls=%async_computation | async-start | bytes 16384 | tf_op jit(solution)/shard_map/all_to_all | solution.py:150
  603.6 1.6 copy-start.4
  603.6 1.6 copy-start.5
  633.0 95.2 %all-to-all-start.4 = ((f32[4,2,16,64,128]{4,3,2,1,0:T(8,128)}), f32[4,2,16,64,128]{4,3,2,1,0:T(8,128)}, u32[]{:S(2)}, u32[]{:S(2)}) async-start(f32[4,2,16,64,128]{4,3,2,1,0:T(8,128)} %bitcast.139), calls=%async_computation.4 | async-start | bytes 8388608 | tf_op jit(solution)/shard_map/all_to_all | solution.py:137
  728.2 7.9 all-to-all-start.1
  736.1 49.1 %all-to-all-start.5 = ((f32[4,2,16,64,128]{4,3,2,0,1:T(8,128)}), f32[4,2,16,64,128]{4,3,2,0,1:T(8,128)}, u32[]{:S(2)}, u32[]{:S(2)}) async-start(f32[4,2,16,64,128]{4,3,2,0,1:T(8,128)} %copy.46), calls=%async_computation.5 | async-start | bytes 8388608 | tf_op jit(solution)/shard_map/all_to_all | solution.py:136
  741.7 982.3 %reduce-scatter.2.cloned.1.call-start = ((), (), s32[]{:S(2)}) async-start(), calls=%async_computation.7 | async-start | bytes 3145728 | tf_op jit(solution)/shard_map/reduce_scatter | solution.py:177
  790.2 933.8 %copy-start.1 = (f32[130816]{0:T(1024)S(1)}, f32[130816]{0:T(1024)}, u32[]{:S(2)}) copy-start(f32[130816]{0:T(1024)} %param.19) | copy-start | bytes 1569796
  1710.6 1.3 copy-start.3
Sparse Core Ops, SparseCore 0:
  1712.1 11.8 reduce-scatter.1
where the time goes:
time: 1750 us; the launch traced here: 1730 us
  loops' own time  498 us (28%)
  local copies, waits for them, and re-layouts  456 us (26%)
  other arithmetic  437 us (25%)
  waiting for transfers between devices  175 us (10%)
  matrix products  120 us (7%)
  starting transfers between devices  30.7 us (2%)
    another operation x1, loops' own time, on_device(): lax.fori_loop(0, arrived, place_one, jnp.zeros((2, FU, FV), jnp.float32))  498 us
    another operation x6, other arithmetic  410 us
    dynamic_update_slice x128, local copies, waits for them, and re-layouts, place_one(): lax.dynamic_update_slice(partial_value, before + both, (anchor, offset_u,...  219 us
    squeeze x128, local copies, waits for them, and re-layouts, place_one(): piece = recv_grid[item]  98.2 us
    all_to_all x1, waiting for transfers between devices, on_device(): lax.all_to_all(send_grid.reshape(n_col, n_row, sub_cap, SG, 2 * SG), 'col...  89.7 us
    dynamic_slice x128, local copies, waits for them, and re-layouts, place_one(): offset_v = recv_offsets[item, 1]  83.5 us
    dot_general x6, matrix products, grid_group(): jnp.einsum('gkx,gky->gxy', left_side, right_side, preferred_element_type=...  82.7 us
    all_to_all x1, waiting for transfers between devices, on_device(): lax.all_to_all(lax.all_to_all(send_grid.reshape(n_col, n_row, sub_cap, SG...  42 us
  transfers between devices with their start and end apart: 7, of which 4 were waited for; matrix products, arithmetic and copies ran while one was open for 34% of the time, Pallas kernels for 0%

commit v1 on v0

v1 whole, which is shorter than its diff:
```python
import functools
import math

import jax
import jax.numpy as jnp
import numpy as np
from jax import lax
from jax.experimental import pallas as pl
from jax.experimental.pallas import tpu as pltpu
from jax.sharding import PartitionSpec as P

SG = 64
BV = 256
FU = 512
FV = 512
LANES = 128
TILES = FV // LANES
UNROLL = 4
FFT_UNROLL = 4
BIG = 1 << 30


def _poly(fn, terms):
    y = np.cos(np.pi * (np.arange(400) + 0.5) / 400)
    s = 0.25 * 0.5 * (y + 1.0)
    fit = np.polynomial.chebyshev.Chebyshev.fit(s, fn(np.sqrt(s)), terms - 1, domain=[0.0, 0.25])
    return [float(c) for c in fit.convert(kind=np.polynomial.Polynomial, domain=[-1, 1]).coef]


COS_COEF = _poly(lambda t: np.cos(2 * np.pi * t), 8)
SIN_COEF = _poly(lambda t: np.sin(2 * np.pi * t) / t, 7)


def _horner(coef, s):
    out = jnp.full_like(s, coef[-1])
    for c in coef[-2::-1]:
        out = out * s + c
    return out


def _fine(turns, steps):
    t = turns * steps
    t = t - jnp.round(t)
    s = t * t
    return _horner(COS_COEF, s), t * _horner(SIN_COEF, s)


def _powers(turns, steps, scale):
    er, ei = _fine(turns, steps)
    z4r = jnp.broadcast_to(er[4:5], er.shape)
    z4i = jnp.broadcast_to(ei[4:5], ei.shape)

    def square(r, i):
        return r * r - i * i, 2.0 * (r * i)

    z1 = square(z4r, z4i)
    z2 = square(*z1)
    z3 = (z1[0] * z2[0] - z1[1] * z2[1], z1[0] * z2[1] + z1[1] * z2[0])
    z4 = square(*z2)
    if scale is not None:
        wr, wi = scale
        er, ei = er * wr - ei * wi, er * wi + ei * wr
    real = [None] * 8
    imag = [None] * 8
    real[4], imag[4] = er, ei
    for a, (zr, zi) in ((1, z1), (2, z2), (3, z3), (4, z4)):
        rr, ii, ri, ir = er * zr, ei * zi, er * zi, ei * zr
        real[4 - a], imag[4 - a] = rr + ii, ir - ri
        if a < 4:
            real[4 + a], imag[4 + a] = rr - ii, ri + ir
    return jnp.concatenate(real + imag, axis=0).astype(jnp.bfloat16)


def _block_product(block_ref, index, steps):
    left, right = [], []
    for h in range(2):
        def row(k):
            return jnp.broadcast_to(block_ref[index, 2 * k + h : 2 * k + h + 1, :], (8, LANES))

        left.append(_powers(row(2), steps, (row(0), row(1))))
        right.append(_powers(row(3), steps, None))
    return lax.dot_general(
        jnp.concatenate(left, axis=1),
        jnp.concatenate(right, axis=1),
        (((1,), (1,)), ((), ())),
        preferred_element_type=jnp.float32,
    )


def _split(x):
    hi = x.astype(jnp.bfloat16)
    lo = (x - hi.astype(jnp.float32)).astype(jnp.bfloat16)
    return hi, lo


def _combine(four, sign):
    return four[:SG] + pltpu.roll(four[SG:], SG, 1) * sign


def facet_kernel(
    shift,
    subs,
    count_ref,
    keys_ref,
    place_ref,
    vis_ref,
    block_ref,
    screen_a_ref,
    screen_b_ref,
    right_ref,
    left_ref,
    mine_ref,
    theirs_ref,
    sums,
    facet,
    found,
):
    trash = sums.shape[0] - 1
    steps = lax.broadcasted_iota(jnp.int32, (8, LANES), 0).astype(jnp.float32)
    lane = lax.broadcasted_iota(jnp.int32, (SG, LANES), 1)
    sign = jnp.where(lane < SG, -1.0, 1.0)
    facet[...] = jnp.zeros_like(facet)
    count = count_ref[0]

    def grid_blocks(step, carry):
        last_sub, slot = carry
        jobs = []
        for k in range(UNROLL):
            at = step * UNROLL + k
            key = keys_ref[at]
            real = at < count
            index = jnp.where(real, key & ((1 << shift) - 1), 0)
            sub = jnp.where(real, key >> shift, last_sub)
            fresh = sub != last_sub
            slot = slot + fresh.astype(jnp.int32)
            last_sub = sub
            found[jnp.maximum(slot, 0)] = sub
            jobs.append((_block_product(block_ref, index, steps), fresh, jnp.where(real, slot, trash)))
        for product, fresh, where in jobs:
            sums[where] = jnp.where(fresh, 0.0, sums[where]) + product
        return last_sub, slot

    _, top = lax.fori_loop(
        0, (count + UNROLL - 1) // UNROLL, grid_blocks, (jnp.int32(-1), jnp.int32(-1))
    )
    touched = top + 1

    def place_subs(step, carry):
        pieces = []
        for k in range(FFT_UNROLL):
            at = step * FFT_UNROLL + k
            real = at < touched
            at = jnp.minimum(at, touched - 1)
            sub = found[at]
            corner_u, corner_v, plane = place_ref[sub], place_ref[subs + sub], place_ref[2 * subs + sub]
            image = _combine(sums[at], sign)
            masked = image * screen_a_ref[plane] + pltpu.roll(image, SG, 1) * screen_b_ref[plane]
            hi, lo = _split(masked)
            wide = jnp.dot(
                jnp.concatenate([hi, lo], axis=1), right_ref[...], preferred_element_type=jnp.float32
            )
            half = wide[:, :LANES] + wide[:, LANES:]
            hi, lo = _split(half)
            four = jnp.dot(
                left_ref[...],
                jnp.concatenate([hi, lo, hi, jnp.zeros_like(hi)], axis=0),
                preferred_element_type=jnp.float32,
            )
            spectrum = _combine(four, sign)
            off_v = corner_v & (FV - 1)
            pieces.append((spectrum, real, corner_u & (FU - 1), off_v >> 7, off_v & (LANES - 1)))
        for spectrum, real, off_u, tile, s in pieces:
            turned = pltpu.roll(spectrum, s, 1)
            other = pltpu.roll(turned, SG, 1)
            begin = jnp.where(real, s, LANES)
            end = jnp.where(real, s + SG, 0)
            first = (lane >= begin) & (lane < end)
            second = lane < end - LANES
            rows = pl.ds(off_u, SG)
            for part, value in ((0, turned), (1, other)):
                facet[part, tile, rows, :] += jnp.where(first, value, 0.0)
                facet[part, tile + 1, rows, :] += jnp.where(second, value, 0.0)
        return carry

    lax.fori_loop(0, (touched + FFT_UNROLL - 1) // FFT_UNROLL, place_subs, 0)
    half = TILES // 2
    own = vis_ref[0] * half
    far = (1 - vis_ref[0]) * half
    for part in range(2):
        for t in range(half):
            mine_ref[part, :, t * LANES : (t + 1) * LANES] = facet[part, own + t]
            theirs_ref[part, :, t * LANES : (t + 1) * LANES] = facet[part, far + t]


def dft_tables():
    k = np.arange(SG)
    angle = 2.0 * np.pi * (np.outer(k, k) % SG) / SG
    re, im = np.cos(angle), -np.sin(angle)
    right = np.block([[re, im], [-im, re]]) / (SG * math.sqrt(BV))
    left = np.concatenate([re, im], axis=0)

    def split(x):
        hi = np.asarray(x, jnp.bfloat16).astype(np.float64)
        return hi, x - hi

    rhi, rlo = split(right)
    lhi, llo = split(left)
    right = np.block([[rhi, rlo], [rhi, np.zeros_like(rlo)]])
    left = np.concatenate([lhi, lhi, llo, np.zeros_like(llo)], axis=1)
    return jnp.asarray(right, jnp.bfloat16), jnp.asarray(left, jnp.bfloat16)


def on_device(
    visibilities,
    coords,
    block_subgrid,
    baseline_ids,
    live_blocks,
    subgrid_place,
    baseline_weight,
    tapering,
    plane_phase,
):
    nblocks = visibilities.shape[0]
    n_col = lax.axis_size("col")
    n_row = lax.axis_size("row")
    n_vis = lax.axis_size("vis")
    devices = n_col * n_row * n_vis
    facets = n_col * n_row
    sub_dev = subgrid_place.shape[1]
    subs = devices * sub_dev
    held = facets * nblocks
    max_subs = min(devices * (2 * sub_dev // facets), held)
    vis = lax.axis_index("vis")
    live = jnp.arange(nblocks) < live_blocks[0]

    label = jnp.where(live, block_subgrid, -1)
    meta = jnp.concatenate([label, subgrid_place.reshape(-1)])
    meta = lax.all_gather(meta, ("col", "row", "vis"), axis=0, tiled=False)

    weight = jnp.where(live, jnp.take(baseline_weight, baseline_ids), 0.0)
    weighted = visibilities.astype(jnp.float32) * weight[:, None, None]
    payload = jnp.concatenate([weighted, coords], axis=1).reshape(nblocks, 8, LANES)
    blocks = lax.all_gather(payload, ("col", "row"), axis=0, tiled=True)

    labels = lax.dynamic_index_in_dim(
        meta.reshape(facets, n_vis, -1), vis, axis=1, keepdims=False
    )[:, :nblocks].reshape(held)
    place = meta[:, nblocks:].reshape(devices, 3, sub_dev).transpose(1, 0, 2).reshape(3, subs)
    here = (place[0] // FU == lax.axis_index("col")) & (place[1] // FV == lax.axis_index("row"))
    wanted = (labels >= 0) & jnp.take(here, jnp.maximum(labels, 0))
    shift = max(1, (held - 1).bit_length())
    keys = jnp.where(wanted, (labels << shift) + jnp.arange(held, dtype=jnp.int32), BIG)
    keys = jnp.concatenate([lax.sort(keys), jnp.full((UNROLL,), BIG, jnp.int32)])
    count = jnp.sum(wanted.astype(jnp.int32)).reshape(1)

    screen_re = tapering * jnp.cos(plane_phase)
    screen_im = tapering * jnp.sin(plane_phase)
    screen_a = jnp.concatenate([screen_re, screen_re], axis=2)
    screen_b = jnp.concatenate([-screen_im, screen_im], axis=2)
    right, left = dft_tables()

    smem = pl.BlockSpec(memory_space=pltpu.SMEM)
    vmem = pl.BlockSpec(memory_space=pltpu.VMEM)
    half_shape = jax.ShapeDtypeStruct((2, FU, FV // n_vis), jnp.float32)
    mine, theirs = pl.pallas_call(
        functools.partial(facet_kernel, shift, subs),
        out_shape=(half_shape, half_shape),
        in_specs=[smem] * 4 + [vmem] * 5,
        out_specs=(vmem, vmem),
        scratch_shapes=[
            pltpu.VMEM((max_subs + 1, 2 * SG, 2 * SG), jnp.float32),
            pltpu.VMEM((2, TILES + 1, FU, LANES), jnp.float32),
            pltpu.SMEM((max_subs + 8,), jnp.int32),
        ],
        compiler_params=pltpu.CompilerParams(vmem_limit_bytes=56 * 1024 * 1024),
        name="facet",
    )(count, keys, place.reshape(-1), vis.reshape(1), blocks, screen_a, screen_b, right, left)
    swap = [(d, 1 - d) for d in range(n_vis)]
    return mine + lax.ppermute(theirs, "vis", swap)


def solution(mesh):
    spread = ("band", "col", "row", "vis")
    in_specs = (
        P(spread, None, None),
        P(spread, None, None),
        P(spread),
        P(spread),
        P(spread),
        P(None, spread),
        P(),
        P(),
        P(),
    )
    out_specs = P(None, ("band", "col"), ("row", "vis"))
    return jax.shard_map(
        on_device, mesh=mesh, in_specs=in_specs, out_specs=out_specs, check_vma=False
    )
```

time: 1750 us -> 143 us (0.08); the launches traced: 1730 us -> 143 us
  loops' own time: 498 us -> 0 us
  local copies, waits for them, and re-layouts: 456 us -> 11.3 us
  other arithmetic: 437 us -> 13.7 us
  waiting for transfers between devices: 175 us -> 2.89 us
  matrix products: 120 us -> 0 us
  blocking collectives: 0 us -> 58 us
  Pallas kernels: 0 us -> 42.4 us
  starting transfers between devices: 30.7 us -> 0.01 us
    another operation x2 -> x0, loops' own time: 498 us -> none  [the longest x1 498 us: on_device(): lax.fori_loop(0, arrived, place_one, jnp.zeros((2, FU, FV), jnp.float32))]
    another operation x8 -> x0, other arithmetic: 410 us -> none
    dynamic_update_slice x128 -> x0, local copies, waits for them, and re-layouts: 219 us -> none  [place_one(): lax.dynamic_update_slice(partial_value, before + both, (anchor, offset_u,...]
    all_to_all x6 -> x0, waiting for transfers between devices: 163 us -> none  [the longest x1 89.7 us: on_device(): lax.all_to_all(send_grid.reshape(n_col, n_row, sub_cap, SG, 2 * SG), 'col...]
    dot_general x15 -> x0, matrix products: 120 us -> none  [the longest x6 82.7 us: grid_group(): jnp.einsum('gkx,gky->gxy', left_side, right_side, preferred_element_type=...]
    squeeze x134 -> x2, local copies, waits for them, and re-layouts: 104 us -> 0.14 us  [the longest x1 0.07 us: on_device(): place[0] // FU == lax.axis_index('col')]
    dynamic_slice x128 -> x1, local copies, waits for them, and re-layouts: 83.5 us -> 0.01 us  [on_device(): lax.dynamic_index_in_dim(meta.reshape(facets, n_vis, -1), vis, axis=1, ke...]
    unnamed x0 -> x1, blocking collectives: none -> 58 us
  transfers between devices with their start and end apart: 7 -> 2, of which waited for: 4 -> 1; matrix products, arithmetic and copies ran while one was open for 34% -> 12% of each run, Pallas kernels for 0% -> 0%
where the time goes in v1:
time: 143 us
  blocking collectives  58 us (41%)
  Pallas kernels  42.4 us (30%)
  between operations  14.8 us (10%)
  other arithmetic  13.7 us (10%)
  local copies, waits for them, and re-layouts  11.3 us (8%)
  waiting for transfers between devices  2.89 us (2%)
    unnamed x1, blocking collectives  58 us
    pallas_call x1, Pallas kernels, on_device(): pl.pallas_call(functools.partial(facet_kernel, shift, subs), out_shape=(h...  42.4 us
    gather x2, local copies, waits for them, and re-layouts, on_device(): wanted = (labels >= 0) & jnp.take(here, jnp.maximum(labels, 0))  5.08 us
    sort x1, other arithmetic, on_device(): lax.sort(keys)  4.37 us
    ppermute x1, waiting for transfers between devices, on_device(): return mine + lax.ppermute(theirs, 'vis', swap)  2.87 us
  transfers between devices with their start and end apart: 2, of which 1 were waited for; matrix products, arithmetic and copies ran while one was open for 12% of the time, Pallas kernels for 0%

profile of v1, /device:TPU:31, one launch (start us, length us, event | category | flops | bytes accessed | tf_op | source)
XLA Modules:
  0.0 143.0 jit_solution(17074772318229993616)
XLA Ops:
  7.3 0.7 compare_select_fusion
  7.9 1.1 gather_fusion.1
  9.1 0.7 compare_select_fusion.1
  9.8 1.1 convert_multiply_fusion
  10.8 1.1 pad_maximum_fusion
  11.9 0.9 reshape.70
  12.9 0.8 reshape.65
  13.6 1.2 dynamic-slice
  15.5 0.7 compare_select_fusion.2
  16.2 0.2 add_dynamic-update-slice_fusion
  16.3 58.0 %all-reduce.1 = s32[4608]{0:T(1024)S(1)} all-reduce(s32[4608]{0:T(1024)S(1)} %add_dynamic-update-slice_fusion), channel_id=2, replica_groups=mesh['band'=2,'col'=4,'row'=2,'vis'=2] {'col','row','vis'}, use_global_device_ids=true, to_apply=%add.1 | all-reduce | flops 4608 | bytes 36864
  74.3 0.1 reshape.87
  74.4 0.1 reshape.66
  74.5 0.1 slice.23
  74.6 0.1 shift_left.11
  74.7 0.1 reshape.73
  74.7 0.1 reshape.67
  74.8 0.7 reshape_reshape.3.place_ref
  75.5 0.1 squeeze.15
  75.6 0.1 squeeze.16
  75.7 5.0 %gather_fusion = pred[768]{0:T(1024)(128)(4,1)S(1)} fusion(pred[1024]{0:T(1024)(128)(4,1)S(1)} %fusion.6, s32[1024]{0:T(1024)S(1)} %pad_clamp_fusion.1), kind=kCustom, calls=%fused_computation | custom fusion | bytes 4608 | tf_op jit(solution)/shard_map/jit(_take)/gather | solution.py:251
  80.7 0.1 gather.11
  80.8 0.6 convert_reduce_fusion
  81.4 0.1 le.26
  81.5 0.1 ge.23
  81.6 4.4 %sort.14 = (s32[768]{0:T(1024)S(1)}, s32[768]{0:T(1024)}) sort(s32[768]{0:T(1024)S(1)} %add_select_fusion.2, s32[768]{0:T(1024)S(1)} %iota.13), dimensions={0}, to_apply=%region_1.2 | sort | flops 7680 | bytes 12288 | tf_op jit(solution)/shard_map/sort | solution.py:254
  86.0 0.6 concatenate.16.keys_ref
  86.6 1.0 fusion.7
  87.6 1.0 pad_maximum_fusion.1
  88.6 42.4 %facet.1 = (f32[2,512,256]{2,1,0:T(8,128)}, f32[2,512,256]{2,1,0:T(8,128)}) custom-call(s32[1]{0:T(128)} %bitcast.3.count_ref, s32[772]{0:T(1024)} %concatenate.16.keys_ref, s32[3072]{0:T(1024)} %reshape_reshape.3.place_ref, s32[1]{0:T(128)} %bitcast.4.vis_ref, f32[768,8,128]{2,1,0:T(8,128)} %all-gather.3.cloned.1.call-done.block_ref, ...), custom_call_target="tpu_custom_call" | custom-call | tf_op jit(solution)/shard_map/facet/pallas_call | solution.py:266
  130.9 2.9 %collective-permute-done = f32[2,512,256]{2,1,0:T(8,128)S(1)} collective-permute-done((f32[2,512,256]{2,1,0:T(8,128)}, f32[2,512,256]{2,1,0:T(8,128)S(1)}, u32[]{:S(2)}, u32[]{:S(2)}) %collective-permute-start) | collective-permute-done | bytes 1048608 | tf_op jit(solution)/shard_map/ppermute | solution.py:280
  133.8 2.3 %add.30 = f32[2,512,256]{2,1,0:T(8,128)} add(f32[2,512,256]{2,1,0:T(8,128)} %get-tuple-element.10, f32[2,512,256]{2,1,0:T(8,128)S(1)} %collective-permute-done) | non-fusion elementwise | flops 262144 | bytes 3145728 | tf_op jit(solution)/shard_map/add | solution.py:280
  (21 shorter events, 0.1 us)
Async XLA Ops:
  6.5 1.4 copy-start
  6.5 80.1 %copy-start.1 = (f32[8,64,64]{2,1,0:T(8,128)S(1)}, f32[8,64,64]{2,1,0:T(8,128)}, u32[]{:S(2)}) copy-start(f32[8,64,64]{2,1,0:T(8,128)} %param.19) | copy-start | bytes 393220
  6.5 80.1 %copy-start.2 = (f32[64,64]{1,0:T(8,128)S(1)}, f32[64,64]{1,0:T(8,128)}, u32[]{:S(2)}) copy-start(f32[64,64]{1,0:T(8,128)} %param.18) | copy-start | bytes 49156
  6.5 82.0 %all-gather.3.cloned.1.call-start = ((), (), s32[]{:S(2)}) async-start(), calls=%async_computation | async-start | bytes 3538944 | tf_op jit(solution)/shard_map/all_gather | solution.py:244
  130.9 2.9 %collective-permute-start = (f32[2,512,256]{2,1,0:T(8,128)}, f32[2,512,256]{2,1,0:T(8,128)S(1)}, u32[]{:S(2)}, u32[]{:S(2)}) collective-permute-start(f32[2,512,256]{2,1,0:T(8,128)} %get-tuple-element.11), channel_id=1, source_target_pairs={{0,1},{1,0},{2,3},{3,2},{4,5},{5,4},{6,7},{7,6},{8,9},{9,8},{10,11... | collective-permute-start | bytes 3145736 | tf_op jit(solution)/shard_map/ppermute | solution.py:280
Sparse Core Ops, SparseCore 0:
  13.0 59.8 all-gather.2

commit v2 on v1

--- a/solution.py
+++ b/solution.py
@@ -192,6 +192,87 @@
             theirs_ref[part, :, t * LANES : (t + 1) * LANES] = facet[part, far + t]
 
 
+def gather_kernel(n_col, n_row, mine_ref, out_ref, ring_send, ring_recv, row_send, row_recv, own_sem):
+    col, row = lax.axis_index("col"), lax.axis_index("row")
+    right, left = lax.rem(col + 1, n_col), lax.rem(col + n_col - 1, n_col)
+    size = mine_ref.shape[0]
+    mesh_ids = pl.DeviceIdType.MESH
+    barrier = pltpu.get_barrier_semaphore()
+    for peer in (left, right):
+        pl.semaphore_signal(barrier, inc=1, device_id={"col": peer}, device_id_type=mesh_ids)
+    for j in range(1, n_row):
+        pl.semaphore_signal(
+            barrier, inc=1, device_id={"row": lax.rem(row + j, n_row)}, device_id_type=mesh_ids
+        )
+    pl.semaphore_wait(barrier, 1 + n_row)
+
+    def slot(back, at_row):
+        source = lax.rem(col + n_col - back, n_col) * n_row + at_row
+        return out_ref.at[pl.ds(source * size, size)]
+
+    def ring(step):
+        return pltpu.make_async_remote_copy(
+            src_ref=mine_ref if step == 0 else slot(step, row),
+            dst_ref=slot(step, row),
+            send_sem=ring_send.at[step],
+            recv_sem=ring_recv.at[step],
+            device_id={"col": right},
+            device_id_type=mesh_ids,
+        )
+
+    def across(step, j):
+        return pltpu.make_async_remote_copy(
+            src_ref=mine_ref if step == 0 else slot(step, row),
+            dst_ref=slot(step, row),
+            send_sem=row_send.at[step, j - 1],
+            recv_sem=row_recv.at[step, j - 1],
+            device_id={"row": lax.rem(row + j, n_row)},
+            device_id_type=mesh_ids,
+        )
+
+    sent = []
+    for step in range(n_col):
+        if step < n_col - 1:
+            copy = ring(step)
+            copy.start()
+            sent.append(copy)
+        for j in range(1, n_row):
+            side = across(step, j)
+            side.start()
+            sent.append(side)
+        if step == 0:
+            own = pltpu.make_async_copy(mine_ref, slot(0, row), own_sem)
+            own.start()
+        if step < n_col - 1:
+            copy.wait_recv()
+    own.wait()
+    for copy in sent:
+        copy.wait_send()
+    for step in range(n_col):
+        for j in range(1, n_row):
+            across(step, j).wait_recv()
+
+
+def gather_blocks(payload, n_col, n_row):
+    size = payload.shape[0]
+    hbm = pl.BlockSpec(memory_space=pl.ANY)
+    return pl.pallas_call(
+        functools.partial(gather_kernel, n_col, n_row),
+        out_shape=jax.ShapeDtypeStruct((n_col * n_row * size,) + payload.shape[1:], payload.dtype),
+        in_specs=[hbm],
+        out_specs=hbm,
+        scratch_shapes=[
+            pltpu.SemaphoreType.DMA((n_col - 1,)),
+            pltpu.SemaphoreType.DMA((n_col - 1,)),
+            pltpu.SemaphoreType.DMA((n_col, n_row - 1)),
+            pltpu.SemaphoreType.DMA((n_col, n_row - 1)),
+            pltpu.SemaphoreType.DMA,
+        ],
+        compiler_params=pltpu.CompilerParams(collective_id=0, has_side_effects=True),
+        name="gather",
+    )(payload)
+
+
 def dft_tables():
     k = np.arange(SG)
     angle = 2.0 * np.pi * (np.outer(k, k) % SG) / SG
@@ -234,23 +315,31 @@
     vis = lax.axis_index("vis")
     live = jnp.arange(nblocks) < live_blocks[0]
 
+    swap = [(d, n_vis - 1 - d) for d in range(n_vis)]
     label = jnp.where(live, block_subgrid, -1)
-    meta = jnp.concatenate([label, subgrid_place.reshape(-1)])
-    meta = lax.all_gather(meta, ("col", "row", "vis"), axis=0, tiled=False)
+    meta = jnp.concatenate([label, subgrid_place.reshape(-1)]).astype(jnp.float32)
+    meta = jnp.pad(meta, (0, 8 * LANES - meta.shape[0])).reshape(1, 8, LANES)
+    other = lax.ppermute(meta, "vis", swap)
+    pair = jnp.where(vis == 0, jnp.concatenate([meta, other]), jnp.concatenate([other, meta]))
 
     weight = jnp.where(live, jnp.take(baseline_weight, baseline_ids), 0.0)
     weighted = visibilities.astype(jnp.float32) * weight[:, None, None]
     payload = jnp.concatenate([weighted, coords], axis=1).reshape(nblocks, 8, LANES)
-    blocks = lax.all_gather(payload, ("col", "row"), axis=0, tiled=True)
-
-    labels = lax.dynamic_index_in_dim(
-        meta.reshape(facets, n_vis, -1), vis, axis=1, keepdims=False
-    )[:, :nblocks].reshape(held)
-    place = meta[:, nblocks:].reshape(devices, 3, sub_dev).transpose(1, 0, 2).reshape(3, subs)
+    stride = nblocks + n_vis
+    blocks = gather_blocks(jnp.concatenate([payload, pair]), n_col, n_row)
+
+    meta = blocks.reshape(facets, stride, 8, LANES)[:, nblocks:].astype(jnp.int32)
+    meta = meta.reshape(facets, n_vis, 8 * LANES)
+    labels = lax.dynamic_index_in_dim(meta, vis, axis=1, keepdims=False)[:, :nblocks]
+    labels = labels.reshape(held)
+    place = meta.reshape(devices, -1)[:, nblocks : nblocks + 3 * sub_dev]
+    place = place.reshape(devices, 3, sub_dev).transpose(1, 0, 2).reshape(3, subs)
     here = (place[0] // FU == lax.axis_index("col")) & (place[1] // FV == lax.axis_index("row"))
     wanted = (labels >= 0) & jnp.take(here, jnp.maximum(labels, 0))
-    shift = max(1, (held - 1).bit_length())
-    keys = jnp.where(wanted, (labels << shift) + jnp.arange(held, dtype=jnp.int32), BIG)
+    index = jnp.arange(facets)[:, None] * stride + jnp.arange(nblocks)[None, :]
+    index = index.reshape(held).astype(jnp.int32)
+    shift = max(1, (facets * stride - 1).bit_length())
+    keys = jnp.where(wanted, (labels << shift) + index, BIG)
     keys = jnp.concatenate([lax.sort(keys), jnp.full((UNROLL,), BIG, jnp.int32)])
     count = jnp.sum(wanted.astype(jnp.int32)).reshape(1)
 
@@ -276,7 +365,6 @@
         compiler_params=pltpu.CompilerParams(vmem_limit_bytes=56 * 1024 * 1024),
         name="facet",
     )(count, keys, place.reshape(-1), vis.reshape(1), blocks, screen_a, screen_b, right, left)
-    swap = [(d, 1 - d) for d in range(n_vis)]
     return mine + lax.ppermute(theirs, "vis", swap)
 
 

time: 143 us -> 114 us (0.80); the launches traced: 143 us -> 112 us
  blocking collectives: 58 us -> 0 us
  Pallas kernels: 42.4 us -> 78.7 us
  between operations: 14.8 us -> 0.83 us
  starting transfers between devices: 0.01 us -> 4.43 us
  other arithmetic: 13.7 us -> 16.3 us
  local copies, waits for them, and re-layouts: 11.3 us -> 9.18 us
    unnamed x1 -> x0, blocking collectives: 58 us -> none
    pallas_call x0 -> x1, Pallas kernels: none -> 39.6 us  [gather_blocks(): pl.pallas_call(functools.partial(gather_kernel, n_col, n_row), out_shape=...]
    ppermute x1, starting transfers between devices: 0.01 us -> 3.76 us  [on_device(): return mine + lax.ppermute(theirs, 'vis', swap)]
    pallas_call x1, Pallas kernels: 42.4 us -> 39.1 us  [on_device(): pl.pallas_call(functools.partial(facet_kernel, shift, subs), out_shape=(h...]
  transfers between devices with their start and end apart: 2 -> 2, of which waited for: 1 -> 1; matrix products, arithmetic and copies ran while one was open for 12% -> 7% of each run, Pallas kernels for 0% -> 0%
where the time goes in v2:
time: 114 us; the launch traced here: 112 us
  Pallas kernels  78.7 us (69%)
  other arithmetic  16.3 us (14%)
  local copies, waits for them, and re-layouts  9.18 us (8%)
  starting transfers between devices  4.43 us (4%)
  waiting for transfers between devices  2.5 us (2%)
    pallas_call x1, Pallas kernels, gather_blocks(): pl.pallas_call(functools.partial(gather_kernel, n_col, n_row), out_shape=...  39.6 us
    pallas_call x1, Pallas kernels, on_device(): pl.pallas_call(functools.partial(facet_kernel, shift, subs), out_shape=(h...  39.1 us
    gather x2, local copies, waits for them, and re-layouts, on_device(): wanted = (labels >= 0) & jnp.take(here, jnp.maximum(labels, 0))  5.08 us
    sort x1, other arithmetic, on_device(): lax.sort(keys)  4.37 us
    ppermute x1, starting transfers between devices, on_device(): return mine + lax.ppermute(theirs, 'vis', swap)  3.76 us
    ppermute x1, waiting for transfers between devices, on_device(): return mine + lax.ppermute(theirs, 'vis', swap)  2.5 us
    add x1, other arithmetic, on_device(): return mine + lax.ppermute(theirs, 'vis', swap)  2.33 us
  transfers between devices with their start and end apart: 2, of which 1 were waited for; matrix products, arithmetic and copies ran while one was open for 7% of the time, Pallas kernels for 0%

profile of v2, /device:TPU:31, one launch (start us, length us, event | category | flops | bytes accessed | tf_op | source)
XLA Modules:
  0.0 112.0 jit_solution(12446953128744489590)
XLA Ops:
  0.7 0.8 reshape.82
  1.5 0.7 compare_select_fusion.1
  2.1 0.1 add_convert_fusion
  2.2 0.7 collective-permute-start
  2.9 0.7 compare_select_fusion
  3.6 1.1 %gather_fusion = f32[96]{0:T(128)S(1)} fusion(f32[130816]{0:T(1024)S(1)} %copy-done, s32[1024]{0:T(1024)S(1)} %pad_clamp_fusion.1), kind=kCustom, calls=%fused_computation | custom fusion | bytes 1152 | tf_op jit(solution)/shard_map/jit(_take)/gather | solution.py:325
  4.7 0.7 compare_select_fusion.2
  5.4 1.1 convert_multiply_fusion
  6.5 1.1 pad_maximum_fusion.1
  7.6 1.9 %fusion.7 = (f32[8,64,64]{2,1,0:T(8,128)S(1)}, f32[8,64,64]{2,1,0:T(8,128)S(1)}, f32[8,64,64]{2,1,0:T(8,128)S(1)}) fusion(f32[8,64,64]{2,1,0:T(8,128)} %param.19, f32[64,64]{1,0:T(8,128)} %param.18), kind=kLoop, calls=%fused_computation.48 | loop fusion | flops 98304 | bytes 540672 | tf_op jit(solution)/shard_map/neg | solution.py:349
  9.5 1.0 pad_maximum_fusion.2
  10.5 0.2 reshape.81
  10.7 0.8 pad_maximum_fusion.mine_ref
  11.5 39.6 %gather.18.block_ref = f32[784,8,128]{2,1,0:T(8,128)} custom-call(f32[98,8,128]{2,1,0:T(8,128)} %pad_maximum_fusion.mine_ref), custom_call_target="tpu_custom_call" | custom-call | tf_op jit(solution)/shard_map/gather/pallas_call | solution.py:259
  51.1 0.9 slice_convert_fusion
  52.0 0.1 slice.28
  52.0 0.1 reshape.86
  52.2 0.7 reshape_reshape.7.place_ref
  53.1 0.1 add_add_fusion
  53.2 0.1 add.53
  53.2 0.1 reshape.99
  53.3 5.0 %gather_fusion.1 = pred[768]{0:T(1024)(128)(4,1)S(1)} fusion(pred[1024]{0:T(1024)(128)(4,1)S(1)} %fusion.6, s32[1024]{0:T(1024)S(1)} %pad_clamp_fusion), kind=kCustom, calls=%fused_computation.1 | custom fusion | bytes 4608 | tf_op jit(solution)/shard_map/jit(_take)/gather | solution.py:338
  58.3 0.1 gather.13
  58.4 0.7 convert_reduce_fusion
  59.1 0.1 le.28
  59.2 0.1 ge.24
  59.3 4.4 %sort.14 = (s32[768]{0:T(1024)S(1)}, s32[768]{0:T(1024)}) sort(s32[768]{0:T(1024)S(1)} %and_select_fusion, s32[768]{0:T(1024)S(1)} %iota.19), dimensions={0}, to_apply=%region_1.2 | sort | flops 7680 | bytes 12288 | tf_op jit(solution)/shard_map/sort | solution.py:343
  63.7 0.6 concatenate.29.keys_ref
  64.3 39.1 %facet.1 = (f32[2,512,256]{2,1,0:T(8,128)}, f32[2,512,256]{2,1,0:T(8,128)}) custom-call(s32[1]{0:T(128)} %bitcast.4.count_ref, s32[772]{0:T(1024)} %concatenate.29.keys_ref, s32[3072]{0:T(1024)} %reshape_reshape.7.place_ref, s32[1]{0:T(128)} %bitcast.5.vis_ref, f32[784,8,128]{2,1,0:T(8,128)} %gather.18.block_ref, ...), custom_call_target="tpu_custom_call" | custom-call | tf_op jit(solution)/shard_map/facet/pallas_call | solution.py:355
  103.4 3.8 %collective-permute-start.1 = (f32[2,512,256]{2,1,0:T(8,128)}, f32[2,512,256]{2,1,0:T(8,128)S(1)}, u32[]{:S(2)}, u32[]{:S(2)}) collective-permute-start(f32[2,512,256]{2,1,0:T(8,128)} %get-tuple-element.11), channel_id=1, source_target_pairs={{0,1},{1,0},{2,3},{3,2},{4,5},{5,4},{6,7},{7,6},{8,9},{9,8},{10,11... | collective-permute-start | bytes 3145736 | tf_op jit(solution)/shard_map/ppermute | solution.py:368
  107.2 2.5 %collective-permute-done.1 = f32[2,512,256]{2,1,0:T(8,128)S(1)} collective-permute-done((f32[2,512,256]{2,1,0:T(8,128)}, f32[2,512,256]{2,1,0:T(8,128)S(1)}, u32[]{:S(2)}, u32[]{:S(2)}) %collective-permute-start.1) | collective-permute-done | bytes 1048608 | tf_op jit(solution)/shard_map/ppermute | solution.py:368
  109.7 2.3 %add.54 = f32[2,512,256]{2,1,0:T(8,128)} add(f32[2,512,256]{2,1,0:T(8,128)} %get-tuple-element.10, f32[2,512,256]{2,1,0:T(8,128)S(1)} %collective-permute-done.1) | non-fusion elementwise | flops 262144 | bytes 3145728 | tf_op jit(solution)/shard_map/add | solution.py:368
  (19 shorter events, 0.3 us)
Async XLA Ops:
  0.0 3.6 %copy-start = (f32[130816]{0:T(1024)S(1)}, f32[130816]{0:T(1024)}, u32[]{:S(2)}) copy-start(f32[130816]{0:T(1024)} %param.17) | copy-start | bytes 1569796
  2.2 8.5 %collective-permute-start = (f32[1,8,128]{2,1,0:T(8,128)S(1)}, f32[1,8,128]{2,1,0:T(8,128)S(1)}, u32[]{:S(2)}, u32[]{:S(2)}) collective-permute-start(f32[1,8,128]{2,1,0:T(8,128)S(1)} %pad_bitcast_fusion), channel_id=1, source_target_pairs={{0,1},{1,0},{2,3},{3,2},{4,5},{5,4},{6,7},{7,6},{8,9},{9,8},{10,11... | collective-permute-start | bytes 12296 | tf_op jit(solution)/shard_map/ppermute | solution.py:322
  103.4 6.3 %collective-permute-start.1 = (f32[2,512,256]{2,1,0:T(8,128)}, f32[2,512,256]{2,1,0:T(8,128)S(1)}, u32[]{:S(2)}, u32[]{:S(2)}) collective-permute-start(f32[2,512,256]{2,1,0:T(8,128)} %get-tuple-element.11), channel_id=1, source_target_pairs={{0,1},{1,0},{2,3},{3,2},{4,5},{5,4},{6,7},{7,6},{8,9},{9,8},{10,11... | collective-permute-start | bytes 3145736 | tf_op jit(solution)/shard_map/ppermute | solution.py:368

commit v3 on v2

--- a/solution.py
+++ b/solution.py
@@ -15,8 +15,8 @@
 FV = 512
 LANES = 128
 TILES = FV // LANES
-UNROLL = 4
-FFT_UNROLL = 4
+UNROLL = 16
+FFT_UNROLL = 16
 BIG = 1 << 30
 
 
@@ -177,9 +177,11 @@
             first = (lane >= begin) & (lane < end)
             second = lane < end - LANES
             rows = pl.ds(off_u, SG)
-            for part, value in ((0, turned), (1, other)):
-                facet[part, tile, rows, :] += jnp.where(first, value, 0.0)
-                facet[part, tile + 1, rows, :] += jnp.where(second, value, 0.0)
+            spots = [(part, tile + t, rows) for part in range(2) for t in range(2)]
+            before = [facet[spot] for spot in spots]
+            parts = [jnp.where(m, v, 0.0) for v in (turned, other) for m in (first, second)]
+            for spot, old, new in zip(spots, before, parts):
+                facet[spot] = old + new
         return carry
 
     lax.fori_loop(0, (touched + FFT_UNROLL - 1) // FFT_UNROLL, place_subs, 0)
@@ -192,7 +194,7 @@
             theirs_ref[part, :, t * LANES : (t + 1) * LANES] = facet[part, far + t]
 
 
-def gather_kernel(n_col, n_row, mine_ref, out_ref, ring_send, ring_recv, row_send, row_recv, own_sem):
+def gather_kernel(n_col, n_row, chunks, mine_ref, out_ref, ring_send, ring_recv, row_send, row_recv, own_sem):
     col, row = lax.axis_index("col"), lax.axis_index("row")
     right, left = lax.rem(col + 1, n_col), lax.rem(col + n_col - 1, n_col)
     size = mine_ref.shape[0]
@@ -206,66 +208,94 @@
         )
     pl.semaphore_wait(barrier, 1 + n_row)
 
-    def slot(back, at_row):
+    def slot(back, at_row, k):
         source = lax.rem(col + n_col - back, n_col) * n_row + at_row
-        return out_ref.at[pl.ds(source * size, size)]
-
-    def ring(step):
+        first, count = chunks[k]
+        return out_ref.at[pl.ds(source * size + first, count)]
+
+    def from_here(step, at_row, k):
+        first, count = chunks[k]
+        return mine_ref.at[pl.ds(first, count)] if step == 0 else slot(step, at_row, k)
+
+    def ring(step, j, k):
+        at_row = lax.rem(row + j, n_row)
         return pltpu.make_async_remote_copy(
-            src_ref=mine_ref if step == 0 else slot(step, row),
-            dst_ref=slot(step, row),
-            send_sem=ring_send.at[step],
-            recv_sem=ring_recv.at[step],
+            src_ref=from_here(step, at_row, k) if j == 0 else slot(step, at_row, k),
+            dst_ref=slot(step, at_row, k),
+            send_sem=ring_send.at[step, j, k],
+            recv_sem=ring_recv.at[step, j, k],
             device_id={"col": right},
             device_id_type=mesh_ids,
         )
 
-    def across(step, j):
+    def across(step, j, k):
         return pltpu.make_async_remote_copy(
-            src_ref=mine_ref if step == 0 else slot(step, row),
-            dst_ref=slot(step, row),
-            send_sem=row_send.at[step, j - 1],
-            recv_sem=row_recv.at[step, j - 1],
+            src_ref=from_here(step, row, k),
+            dst_ref=slot(step, row, k),
+            send_sem=row_send.at[step, j - 1, k],
+            recv_sem=row_recv.at[step, j - 1, k],
             device_id={"row": lax.rem(row + j, n_row)},
             device_id_type=mesh_ids,
         )
 
     sent = []
-    for step in range(n_col):
-        if step < n_col - 1:
-            copy = ring(step)
-            copy.start()
-            sent.append(copy)
-        for j in range(1, n_row):
-            side = across(step, j)
-            side.start()
-            sent.append(side)
-        if step == 0:
-            own = pltpu.make_async_copy(mine_ref, slot(0, row), own_sem)
-            own.start()
-        if step < n_col - 1:
-            copy.wait_recv()
+
+    def start(copy):
+        copy.start()
+        sent.append(copy)
+
+    others = range(1, n_row)
+    late = range(1, len(chunks))
+    for j in others:
+        start(across(0, j, 0))
+    for k in range(len(chunks)):
+        start(ring(0, 0, k))
+    own = pltpu.make_async_copy(
+        mine_ref, out_ref.at[pl.ds((col * n_row + row) * size, size)], own_sem
+    )
+    own.start()
+    for k in late:
+        for j in others:
+            start(across(0, j, k))
+    for j in others:
+        across(0, n_row - j, 0).wait_recv()
+        start(ring(0, j, 0))
+    for step in range(1, n_col):
+        for k in late:
+            ring(step - 1, 0, k).wait_recv()
+            if step < n_col - 1:
+                start(ring(step, 0, k))
+            for j in others:
+                start(across(step, j, k))
+        for j in range(n_row):
+            ring(step - 1, j, 0).wait_recv()
+            if step < n_col - 1:
+                start(ring(step, j, 0))
     own.wait()
     for copy in sent:
         copy.wait_send()
     for step in range(n_col):
-        for j in range(1, n_row):
-            across(step, j).wait_recv()
+        for k in late:
+            for j in others:
+                across(step, j, k).wait_recv()
 
 
 def gather_blocks(payload, n_col, n_row):
     size = payload.shape[0]
+    early = size // 6
+    ends = [0] + [early + (size - early) * k // 4 for k in range(5)]
+    chunks = [(ends[k], ends[k + 1] - ends[k]) for k in range(5)]
     hbm = pl.BlockSpec(memory_space=pl.ANY)
     return pl.pallas_call(
-        functools.partial(gather_kernel, n_col, n_row),
+        functools.partial(gather_kernel, n_col, n_row, chunks),
         out_shape=jax.ShapeDtypeStruct((n_col * n_row * size,) + payload.shape[1:], payload.dtype),
         in_specs=[hbm],
         out_specs=hbm,
         scratch_shapes=[
-            pltpu.SemaphoreType.DMA((n_col - 1,)),
-            pltpu.SemaphoreType.DMA((n_col - 1,)),
-            pltpu.SemaphoreType.DMA((n_col, n_row - 1)),
-            pltpu.SemaphoreType.DMA((n_col, n_row - 1)),
+            pltpu.SemaphoreType.DMA((n_col - 1, n_row, 5)),
+            pltpu.SemaphoreType.DMA((n_col - 1, n_row, 5)),
+            pltpu.SemaphoreType.DMA((n_col, n_row - 1, 5)),
+            pltpu.SemaphoreType.DMA((n_col, n_row - 1, 5)),
             pltpu.SemaphoreType.DMA,
         ],
         compiler_params=pltpu.CompilerParams(collective_id=0, has_side_effects=True),
@@ -332,10 +362,13 @@
     meta = meta.reshape(facets, n_vis, 8 * LANES)
     labels = lax.dynamic_index_in_dim(meta, vis, axis=1, keepdims=False)[:, :nblocks]
     labels = labels.reshape(held)
-    place = meta.reshape(devices, -1)[:, nblocks : nblocks + 3 * sub_dev]
-    place = place.reshape(devices, 3, sub_dev).transpose(1, 0, 2).reshape(3, subs)
-    here = (place[0] // FU == lax.axis_index("col")) & (place[1] // FV == lax.axis_index("row"))
-    wanted = (labels >= 0) & jnp.take(here, jnp.maximum(labels, 0))
+    place = meta.reshape(devices, -1)[:, nblocks : nblocks + 3 * sub_dev].reshape(devices, 3, sub_dev)
+    here = (place[:, 0] // FU == lax.axis_index("col")) & (place[:, 1] // FV == lax.axis_index("row"))
+    place = place.transpose(1, 0, 2)
+    owner = (labels[:, None] // sub_dev == jnp.arange(devices)).astype(jnp.float32)
+    local = labels[:, None] % sub_dev == jnp.arange(sub_dev)
+    named = jnp.dot(owner, here.astype(jnp.float32))
+    wanted = (labels >= 0) & (jnp.sum(jnp.where(local, named, 0.0), axis=1) > 0.5)
     index = jnp.arange(facets)[:, None] * stride + jnp.arange(nblocks)[None, :]
     index = index.reshape(held).astype(jnp.int32)
     shift = max(1, (facets * stride - 1).bit_length())

time: 114 us -> 91.2 us (0.80)
  Pallas kernels: 78.7 us -> 65.4 us
  local copies, waits for them, and re-layouts: 9.18 us -> 3.84 us
  starting transfers between devices: 4.43 us -> 1.99 us
    pallas_call x1, Pallas kernels: 39.1 us -> 31.4 us  [on_device(): pl.pallas_call(functools.partial(facet_kernel, shift, subs), out_shape=(h...]
    pallas_call x1, Pallas kernels: 39.6 us -> 34 us  [gather_blocks(): pl.pallas_call(functools.partial(gather_kernel, n_col, n_row, chunks), ou...]
    gather x2 -> x0, local copies, waits for them, and re-layouts: 5.08 us -> none  [on_device(): wanted = (labels >= 0) & jnp.take(here, jnp.maximum(labels, 0))]
    ppermute x1, starting transfers between devices: 3.76 us -> 1.31 us  [on_device(): return mine + lax.ppermute(theirs, 'vis', swap)]
  transfers between devices with their start and end apart: 2 -> 2, of which waited for: 1 -> 1; matrix products, arithmetic and copies ran while one was open for 7% -> 8% of each run, Pallas kernels for 0% -> 0%
where the time goes in v3:
time: 91.2 us; the launch traced here: 90.3 us
  Pallas kernels  65.4 us (72%)
  other arithmetic  15.4 us (17%)
  local copies, waits for them, and re-layouts  3.84 us (4%)
  waiting for transfers between devices  2.5 us (3%)
  starting transfers between devices  1.99 us (2%)
    pallas_call x1, Pallas kernels, gather_blocks(): pl.pallas_call(functools.partial(gather_kernel, n_col, n_row, chunks), ou...  34 us
    pallas_call x1, Pallas kernels, on_device(): pl.pallas_call(functools.partial(facet_kernel, shift, subs), out_shape=(h...  31.4 us
    sort x1, other arithmetic, on_device(): lax.sort(keys)  4.37 us
    ppermute x1, waiting for transfers between devices, on_device(): return mine + lax.ppermute(theirs, 'vis', swap)  2.5 us
    add x1, other arithmetic, on_device(): return mine + lax.ppermute(theirs, 'vis', swap)  2.33 us
    neg x1, other arithmetic, on_device(): screen_b = jnp.concatenate([-screen_im, screen_im], axis=2)  1.92 us
  transfers between devices with their start and end apart: 2, of which 1 were waited for; matrix products, arithmetic and copies ran while one was open for 8% of the time, Pallas kernels for 0%

profile of v3, /device:TPU:31, one launch (start us, length us, event | category | flops | bytes accessed | tf_op | source)
XLA Modules:
  0.0 90.3 jit_solution(6289646075752949052)
XLA Ops:
  0.7 0.8 reshape.142
  1.5 0.7 compare_select_fusion.1
  2.1 0.1 add_convert_fusion
  2.2 0.7 collective-permute-start
  2.9 0.7 compare_select_fusion
  3.6 0.1 iota_add_fusion
  3.7 1.1 %gather_fusion = f32[96]{0:T(128)S(1)} fusion(f32[130816]{0:T(1024)S(1)} %copy-done, s32[1024]{0:T(1024)S(1)} %pad_clamp_fusion), kind=kCustom, calls=%fused_computation | custom fusion | bytes 1152 | tf_op jit(solution)/shard_map/jit(_take)/gather | solution.py:355
  4.8 0.7 compare_select_fusion.2
  5.5 1.1 %convert_multiply_fusion = f32[96,2,256]{2,1,0:T(2,128)S(1)} fusion(bf16[96,2,256]{2,1,0:T(2,128)(2,1)} %param.11, f32[96]{0:T(128)S(1)} %compare_select_fusion.2), kind=kLoop, calls=%fused_computation.12 | loop fusion | flops 98304 | bytes 295296 | tf_op jit(solution)/shard_map/mul | solution.py:356
  6.5 1.9 %fusion.25 = (f32[8,64,64]{2,1,0:T(8,128)S(1)}, f32[8,64,64]{2,1,0:T(8,128)S(1)}, f32[8,64,64]{2,1,0:T(8,128)S(1)}) fusion(f32[8,64,64]{2,1,0:T(8,128)} %param.19, f32[64,64]{1,0:T(8,128)} %param.18), kind=kLoop, calls=%fused_computation.67 | loop fusion | flops 98304 | bytes 540672 | tf_op jit(solution)/shard_map/neg | solution.py:382
  8.5 1.0 %pad_maximum_fusion.2 = (f32[8,64,128]{2,1,0:T(8,128)}, f32[8,64,128]{2,1,0:T(8,128)}) fusion(f32[8,64,64]{2,1,0:T(8,128)S(1)} %get-tuple-element.16, f32[8,64,64]{2,1,0:T(8,128)S(1)} %get-tuple-element.13, f32[8,64,64]{2,1,0:T(8,128)S(1)} %get-tuple-element.12), kind=kLoop, calls=%fused_computation.6 | loop fusion | flops 131072 | bytes 917504 | tf_op jit(solution)/shard_map/concatenate | solution.py:381
  9.5 0.0 copy-done.1
  9.5 0.2 pad_maximum_fusion.1
  9.7 0.1 add.65
  9.7 0.2 reshape.141
  9.9 0.0 collective-permute-done
  9.9 0.8 pad_maximum_fusion.mine_ref
  10.7 34.0 %gather.8.block_ref = f32[784,8,128]{2,1,0:T(8,128)} custom-call(f32[98,8,128]{2,1,0:T(8,128)} %pad_maximum_fusion.mine_ref), custom_call_target="tpu_custom_call" | custom-call | tf_op jit(solution)/shard_map/gather/pallas_call | solution.py:289
  44.7 0.9 slice_convert_fusion
  45.6 0.1 slice.24
  45.7 0.1 reshape.146
  45.8 0.7 reshape.148.place_ref
  46.5 0.1 broadcast_in_dim_reshape.4
  46.6 0.4 fusion
  47.0 0.1 gt.12
  47.1 0.7 convert_reduce_fusion
  47.8 4.4 %sort.14 = (s32[768]{0:T(1024)S(1)}, s32[768]{0:T(1024)}) sort(s32[768]{0:T(1024)S(1)} %get-tuple-element.14, s32[768]{0:T(1024)S(1)} %iota.27), dimensions={0}, to_apply=%region_2.3 | sort | flops 7680 | bytes 12288 | tf_op jit(solution)/shard_map/sort | solution.py:376
  52.1 0.6 concatenate.29.keys_ref
  52.7 31.4 %facet.1 = (f32[2,512,256]{2,1,0:T(8,128)}, f32[2,512,256]{2,1,0:T(8,128)}) custom-call(s32[1]{0:T(128)} %bitcast.5.count_ref, s32[784]{0:T(1024)} %concatenate.29.keys_ref, s32[3072]{0:T(1024)} %reshape.148.place_ref, s32[1]{0:T(128)} %bitcast.7.vis_ref, f32[784,8,128]{2,1,0:T(8,128)} %gather.8.block_ref, f32[8,64,128]{2,1,0:T(8,128)} %get-tuple-element.21.screen_a_ref, ...), custom_call_target="tpu_custom_call" | custom-call | tf_op jit(solution)/shard_map/facet/pallas_call | solution.py:388
  84.1 1.3 %collective-permute-start.1 = (f32[2,512,256]{2,1,0:T(8,128)}, f32[2,512,256]{2,1,0:T(8,128)S(1)}, u32[]{:S(2)}, u32[]{:S(2)}) collective-permute-start(f32[2,512,256]{2,1,0:T(8,128)} %get-tuple-element.11), channel_id=1, source_target_pairs={{0,1},{1,0},{2,3},{3,2},{4,5},{5,4},{6,7},{7,6},{8,9},{9,8},{10,11... | collective-permute-start | bytes 3145736 | tf_op jit(solution)/shard_map/ppermute | solution.py:401
  85.5 2.5 %collective-permute-done.1 = f32[2,512,256]{2,1,0:T(8,128)S(1)} collective-permute-done((f32[2,512,256]{2,1,0:T(8,128)}, f32[2,512,256]{2,1,0:T(8,128)S(1)}, u32[]{:S(2)}, u32[]{:S(2)}) %collective-permute-start.1) | collective-permute-done | bytes 1048608 | tf_op jit(solution)/shard_map/ppermute | solution.py:401
  88.0 2.3 %add.67 = f32[2,512,256]{2,1,0:T(8,128)} add(f32[2,512,256]{2,1,0:T(8,128)} %get-tuple-element.10, f32[2,512,256]{2,1,0:T(8,128)S(1)} %collective-permute-done.1) | non-fusion elementwise | flops 262144 | bytes 3145728 | tf_op jit(solution)/shard_map/add | solution.py:401
  (17 shorter events, 0.2 us)
Async XLA Ops:
  0.0 3.7 %copy-start = (f32[130816]{0:T(1024)S(1)}, f32[130816]{0:T(1024)}, u32[]{:S(2)}) copy-start(f32[130816]{0:T(1024)} %param.17) | copy-start | bytes 1569796
  0.0 9.5 %copy-start.1 = (f32[96,2,256]{2,1,0:T(2,128)S(1)}, f32[96,2,256]{2,1,0:T(2,128)}, u32[]{:S(2)}) copy-start(f32[96,2,256]{2,1,0:T(2,128)} %param.12) | copy-start | bytes 589828
  2.2 7.7 %collective-permute-start = (f32[1,8,128]{2,1,0:T(8,128)S(1)}, f32[1,8,128]{2,1,0:T(8,128)S(1)}, u32[]{:S(2)}, u32[]{:S(2)}) collective-permute-start(f32[1,8,128]{2,1,0:T(8,128)S(1)} %pad_bitcast_fusion), channel_id=1, source_target_pairs={{0,1},{1,0},{2,3},{3,2},{4,5},{5,4},{6,7},{7,6},{8,9},{9,8},{10,11... | collective-permute-start | bytes 12296 | tf_op jit(solution)/shard_map/ppermute | solution.py:352
  84.1 3.8 %collective-permute-start.1 = (f32[2,512,256]{2,1,0:T(8,128)}, f32[2,512,256]{2,1,0:T(8,128)S(1)}, u32[]{:S(2)}, u32[]{:S(2)}) collective-permute-start(f32[2,512,256]{2,1,0:T(8,128)} %get-tuple-element.11), channel_id=1, source_target_pairs={{0,1},{1,0},{2,3},{3,2},{4,5},{5,4},{6,7},{7,6},{8,9},{9,8},{10,11... | collective-permute-start | bytes 3145736 | tf_op jit(solution)/shard_map/ppermute | solution.py:401

commit v4 on v3

--- a/solution.py
+++ b/solution.py
@@ -127,7 +127,7 @@
         jobs = []
         for k in range(UNROLL):
             at = step * UNROLL + k
-            key = keys_ref[at]
+            key = keys_ref[jnp.minimum(at, keys_ref.shape[0] - 1)]
             real = at < count
             index = jnp.where(real, key & ((1 << shift) - 1), 0)
             sub = jnp.where(real, key >> shift, last_sub)
@@ -373,7 +373,7 @@
     index = index.reshape(held).astype(jnp.int32)
     shift = max(1, (facets * stride - 1).bit_length())
     keys = jnp.where(wanted, (labels << shift) + index, BIG)
-    keys = jnp.concatenate([lax.sort(keys), jnp.full((UNROLL,), BIG, jnp.int32)])
+    keys = lax.sort(keys, is_stable=False)
     count = jnp.sum(wanted.astype(jnp.int32)).reshape(1)
 
     screen_re = tapering * jnp.cos(plane_phase)

time: 91.2 us -> 93.8 us (1.029); the launches traced: 90.3 us -> 95.2 us
  starting transfers between devices: 1.99 us -> 8.69 us
  Pallas kernels: 65.4 us -> 64.3 us
    ppermute x1, starting transfers between devices: 1.31 us -> 8.02 us  [on_device(): return mine + lax.ppermute(theirs, 'vis', swap)]
    pallas_call x1, Pallas kernels: 31.4 us -> 30.4 us  [on_device(): pl.pallas_call(functools.partial(facet_kernel, shift, subs), out_shape=(h...]
  transfers between devices with their start and end apart: 2 -> 2, of which waited for: 1 -> 1; matrix products, arithmetic and copies ran while one was open for 8% -> 7% of each run, Pallas kernels for 0% -> 0%
where the time goes in v4:
time: 93.8 us; the launch traced here: 95.2 us
  Pallas kernels  64.3 us (69%)
  other arithmetic  15.2 us (16%)
  starting transfers between devices  8.69 us (9%)
  local copies, waits for them, and re-layouts  3.24 us (3%)
  waiting for transfers between devices  2.5 us (3%)
    pallas_call x1, Pallas kernels, gather_blocks(): pl.pallas_call(functools.partial(gather_kernel, n_col, n_row, chunks), ou...  34 us
    pallas_call x1, Pallas kernels, on_device(): pl.pallas_call(functools.partial(facet_kernel, shift, subs), out_shape=(h...  30.4 us
    ppermute x1, starting transfers between devices, on_device(): return mine + lax.ppermute(theirs, 'vis', swap)  8.02 us
    sort x1, other arithmetic, on_device(): keys = lax.sort(keys, is_stable=False)  4.23 us
    ppermute x1, waiting for transfers between devices, on_device(): return mine + lax.ppermute(theirs, 'vis', swap)  2.5 us
    add x1, other arithmetic, on_device(): return mine + lax.ppermute(theirs, 'vis', swap)  2.33 us
    neg x1, other arithmetic, on_device(): screen_b = jnp.concatenate([-screen_im, screen_im], axis=2)  1.92 us
  transfers between devices with their start and end apart: 2, of which 1 were waited for; matrix products, arithmetic and copies ran while one was open for 7% of the time, Pallas kernels for 0%

profile of v4, /device:TPU:31, one launch (start us, length us, event | category | flops | bytes accessed | tf_op | source)
XLA Modules:
  0.0 95.2 jit_solution(14579272238814212172)
XLA Ops:
  0.0 0.0 copy-start
  0.7 0.8 reshape.142
  1.5 0.7 compare_select_fusion.1
  2.1 0.1 add_convert_fusion
  2.2 0.7 collective-permute-start
  2.9 0.7 compare_select_fusion
  3.6 0.1 iota_add_fusion
  3.6 0.0 copy-done
  3.7 1.1 %gather_fusion = f32[96]{0:T(128)S(1)} fusion(f32[130816]{0:T(1024)S(1)} %copy-done, s32[1024]{0:T(1024)S(1)} %pad_clamp_fusion), kind=kCustom, calls=%fused_computation | custom fusion | bytes 1152 | tf_op jit(solution)/shard_map/jit(_take)/gather | solution.py:355
  4.8 0.7 compare_select_fusion.2
  5.5 1.1 %convert_multiply_fusion = f32[96,2,256]{2,1,0:T(2,128)S(1)} fusion(bf16[96,2,256]{2,1,0:T(2,128)(2,1)} %param.11, f32[96]{0:T(128)S(1)} %compare_select_fusion.2), kind=kLoop, calls=%fused_computation.12 | loop fusion | flops 98304 | bytes 295296 | tf_op jit(solution)/shard_map/mul | solution.py:356
  6.5 1.9 %fusion.25 = (f32[8,64,64]{2,1,0:T(8,128)S(1)}, f32[8,64,64]{2,1,0:T(8,128)S(1)}, f32[8,64,64]{2,1,0:T(8,128)S(1)}) fusion(f32[8,64,64]{2,1,0:T(8,128)} %param.19, f32[64,64]{1,0:T(8,128)} %param.18), kind=kLoop, calls=%fused_computation.67 | loop fusion | flops 98304 | bytes 540672 | tf_op jit(solution)/shard_map/neg | solution.py:382
  8.5 1.0 %pad_maximum_fusion.2 = (f32[8,64,128]{2,1,0:T(8,128)}, f32[8,64,128]{2,1,0:T(8,128)}) fusion(f32[8,64,64]{2,1,0:T(8,128)S(1)} %get-tuple-element.13, f32[8,64,64]{2,1,0:T(8,128)S(1)} %get-tuple-element.10, f32[8,64,64]{2,1,0:T(8,128)S(1)} %get-tuple-element.9), kind=kLoop, calls=%fused_computation.6 | loop fusion | flops 131072 | bytes 917504 | tf_op jit(solution)/shard_map/concatenate | solution.py:381
  9.5 0.2 pad_maximum_fusion.1
  9.7 0.1 add.63
  9.8 0.2 reshape.141
  9.9 0.0 collective-permute-done
  9.9 0.8 pad_maximum_fusion.mine_ref
  10.7 34.0 %gather.8.block_ref = f32[784,8,128]{2,1,0:T(8,128)} custom-call(f32[98,8,128]{2,1,0:T(8,128)} %pad_maximum_fusion.mine_ref), custom_call_target="tpu_custom_call" | custom-call | tf_op jit(solution)/shard_map/gather/pallas_call | solution.py:289
  44.7 0.9 slice_convert_fusion
  45.6 0.1 slice.24
  45.7 0.1 reshape.146
  45.8 0.7 reshape.148.place_ref
  46.5 0.1 broadcast_in_dim_reshape.4
  46.6 0.4 fusion
  47.0 4.2 %sort.7.keys_ref = s32[768]{0:T(1024)} sort(s32[768]{0:T(1024)S(1)} %get-tuple-element.11), dimensions={0}, to_apply=%region_2.3 | sort | flops 7680 | bytes 6144 | tf_op jit(solution)/shard_map/sort | solution.py:376
  51.2 0.1 gt.12
  51.3 0.7 convert_reduce_fusion
  52.0 30.4 %facet.1 = (f32[2,512,256]{2,1,0:T(8,128)}, f32[2,512,256]{2,1,0:T(8,128)}) custom-call(s32[1]{0:T(128)} %bitcast.5.count_ref, s32[768]{0:T(1024)} %sort.7.keys_ref, s32[3072]{0:T(1024)} %reshape.148.place_ref, s32[1]{0:T(128)} %bitcast.7.vis_ref, f32[784,8,128]{2,1,0:T(8,128)} %gather.8.block_ref, f32[8,64,128]{2,1,0:T(8,128)} %get-tuple-element.18.screen_a_ref, ...), custom_call_target="tpu_custom_call" | custom-call | tf_op jit(solution)/shard_map/facet/pallas_call | solution.py:388
  82.4 8.0 %collective-permute-start.1 = (f32[2,512,256]{2,1,0:T(8,128)}, f32[2,512,256]{2,1,0:T(8,128)S(1)}, u32[]{:S(2)}, u32[]{:S(2)}) collective-permute-start(f32[2,512,256]{2,1,0:T(8,128)} %get-tuple-element.8), channel_id=1, source_target_pairs={{0,1},{1,0},{2,3},{3,2},{4,5},{5,4},{6,7},{7,6},{8,9},{9,8},{10,11... | collective-permute-start | bytes 3145736 | tf_op jit(solution)/shard_map/ppermute | solution.py:401
  90.4 2.5 %collective-permute-done.1 = f32[2,512,256]{2,1,0:T(8,128)S(1)} collective-permute-done((f32[2,512,256]{2,1,0:T(8,128)}, f32[2,512,256]{2,1,0:T(8,128)S(1)}, u32[]{:S(2)}, u32[]{:S(2)}) %collective-permute-start.1) | collective-permute-done | bytes 1048608 | tf_op jit(solution)/shard_map/ppermute | solution.py:401
  92.9 2.3 %add.65 = f32[2,512,256]{2,1,0:T(8,128)} add(f32[2,512,256]{2,1,0:T(8,128)} %get-tuple-element.7, f32[2,512,256]{2,1,0:T(8,128)S(1)} %collective-permute-done.1) | non-fusion elementwise | flops 262144 | bytes 3145728 | tf_op jit(solution)/shard_map/add | solution.py:401
  (15 shorter events, 0.2 us)
Async XLA Ops:
  0.0 3.7 %copy-start = (f32[130816]{0:T(1024)S(1)}, f32[130816]{0:T(1024)}, u32[]{:S(2)}) copy-start(f32[130816]{0:T(1024)} %param.17) | copy-start | bytes 1569796
  0.0 9.5 %copy-start.1 = (f32[96,2,256]{2,1,0:T(2,128)S(1)}, f32[96,2,256]{2,1,0:T(2,128)}, u32[]{:S(2)}) copy-start(f32[96,2,256]{2,1,0:T(2,128)} %param.12) | copy-start | bytes 589828
  2.2 7.7 %collective-permute-start = (f32[1,8,128]{2,1,0:T(8,128)S(1)}, f32[1,8,128]{2,1,0:T(8,128)S(1)}, u32[]{:S(2)}, u32[]{:S(2)}) collective-permute-start(f32[1,8,128]{2,1,0:T(8,128)S(1)} %pad_bitcast_fusion), channel_id=1, source_target_pairs={{0,1},{1,0},{2,3},{3,2},{4,5},{5,4},{6,7},{7,6},{8,9},{9,8},{10,11... | collective-permute-start | bytes 12296 | tf_op jit(solution)/shard_map/ppermute | solution.py:352
  82.4 10.5 %collective-permute-start.1 = (f32[2,512,256]{2,1,0:T(8,128)}, f32[2,512,256]{2,1,0:T(8,128)S(1)}, u32[]{:S(2)}, u32[]{:S(2)}) collective-permute-start(f32[2,512,256]{2,1,0:T(8,128)} %get-tuple-element.8), channel_id=1, source_target_pairs={{0,1},{1,0},{2,3},{3,2},{4,5},{5,4},{6,7},{7,6},{8,9},{9,8},{10,11... | collective-permute-start | bytes 3145736 | tf_op jit(solution)/shard_map/ppermute | solution.py:401

commit v5 on v4

--- a/solution.py
+++ b/solution.py
@@ -352,7 +352,7 @@
     other = lax.ppermute(meta, "vis", swap)
     pair = jnp.where(vis == 0, jnp.concatenate([meta, other]), jnp.concatenate([other, meta]))
 
-    weight = jnp.where(live, jnp.take(baseline_weight, baseline_ids), 0.0)
+    weight = jnp.where(live, baseline_weight.at[baseline_ids].get(mode="promise_in_bounds"), 0.0)
     weighted = visibilities.astype(jnp.float32) * weight[:, None, None]
     payload = jnp.concatenate([weighted, coords], axis=1).reshape(nblocks, 8, LANES)
     stride = nblocks + n_vis

time: 93.8 us -> 90.9 us (0.969); the launches traced: 95.2 us -> 90.1 us
  starting transfers between devices: 8.69 us -> 4.18 us
    ppermute x1, starting transfers between devices: 8.02 us -> 3.5 us  [on_device(): return mine + lax.ppermute(theirs, 'vis', swap)]
where the time goes in v5:
time: 90.9 us; the launch traced here: 90.1 us
  Pallas kernels  64.3 us (71%)
  other arithmetic  14.6 us (16%)
  starting transfers between devices  4.18 us (5%)
  local copies, waits for them, and re-layouts  3.24 us (4%)
  waiting for transfers between devices  2.5 us (3%)
    pallas_call x1, Pallas kernels, gather_blocks(): pl.pallas_call(functools.partial(gather_kernel, n_col, n_row, chunks), ou...  34 us
    pallas_call x1, Pallas kernels, on_device(): pl.pallas_call(functools.partial(facet_kernel, shift, subs), out_shape=(h...  30.4 us
    sort x1, other arithmetic, on_device(): keys = lax.sort(keys, is_stable=False)  4.23 us
    ppermute x1, starting transfers between devices, on_device(): return mine + lax.ppermute(theirs, 'vis', swap)  3.5 us
    ppermute x1, waiting for transfers between devices, on_device(): return mine + lax.ppermute(theirs, 'vis', swap)  2.5 us
    add x1, other arithmetic, on_device(): return mine + lax.ppermute(theirs, 'vis', swap)  2.33 us
    neg x1, other arithmetic, on_device(): screen_b = jnp.concatenate([-screen_im, screen_im], axis=2)  1.92 us
  transfers between devices with their start and end apart: 2, of which 1 were waited for; matrix products, arithmetic and copies ran while one was open for 7% of the time, Pallas kernels for 0%

profile of v5, /device:TPU:31, one launch (start us, length us, event | category | flops | bytes accessed | tf_op | source)
XLA Modules:
  0.0 90.1 jit_solution(8983053429594607071)
XLA Ops:
  0.0 0.0 copy-start
  0.7 0.8 reshape.136
  1.5 0.7 compare_select_fusion.1
  2.1 0.1 add_convert_fusion
  2.2 0.7 collective-permute-start
  2.9 0.7 compare_select_fusion
  3.6 0.1 iota_add_fusion
  3.6 0.0 copy-done
  3.7 1.1 %gather_fusion = f32[96]{0:T(128)S(1)} fusion(f32[130816]{0:T(1024)S(1)} %copy-done, s32[1024]{0:T(1024)S(1)} %pad_clamp_fusion), kind=kCustom, calls=%fused_computation | custom fusion | bytes 1152 | tf_op jit(solution)/shard_map/gather | solution.py:355
  4.8 1.1 %convert_multiply_fusion = f32[96,2,256]{2,1,0:T(2,128)S(1)} fusion(bf16[96,2,256]{2,1,0:T(2,128)(2,1)} %param.11, f32[96]{0:T(128)S(1)} %compare_select_fusion.2), kind=kLoop, calls=%fused_computation.12 | loop fusion | flops 98304 | bytes 295296 | tf_op jit(solution)/shard_map/mul | solution.py:356
  5.9 1.9 %fusion.25 = (f32[8,64,64]{2,1,0:T(8,128)S(1)}, f32[8,64,64]{2,1,0:T(8,128)S(1)}, f32[8,64,64]{2,1,0:T(8,128)S(1)}) fusion(f32[8,64,64]{2,1,0:T(8,128)} %param.19, f32[64,64]{1,0:T(8,128)} %param.18), kind=kLoop, calls=%fused_computation.66 | loop fusion | flops 98304 | bytes 540672 | tf_op jit(solution)/shard_map/neg | solution.py:382
  7.8 1.0 %pad_maximum_fusion.2 = (f32[8,64,128]{2,1,0:T(8,128)}, f32[8,64,128]{2,1,0:T(8,128)}) fusion(f32[8,64,64]{2,1,0:T(8,128)S(1)} %get-tuple-element.13, f32[8,64,64]{2,1,0:T(8,128)S(1)} %get-tuple-element.10, f32[8,64,64]{2,1,0:T(8,128)S(1)} %get-tuple-element.9), kind=kLoop, calls=%fused_computation.6 | loop fusion | flops 131072 | bytes 917504 | tf_op jit(solution)/shard_map/concatenate | solution.py:381
  8.8 0.0 copy-done.1
  8.8 0.2 pad_maximum_fusion.1
  9.0 0.1 add.61
  9.1 0.2 reshape.135
  9.3 0.0 collective-permute-done
  9.3 0.8 pad_maximum_fusion.mine_ref
  10.1 34.0 %gather.7.block_ref = f32[784,8,128]{2,1,0:T(8,128)} custom-call(f32[98,8,128]{2,1,0:T(8,128)} %pad_maximum_fusion.mine_ref), custom_call_target="tpu_custom_call" | custom-call | tf_op jit(solution)/shard_map/gather/pallas_call | solution.py:289
  44.0 0.9 slice_convert_fusion
  45.0 0.1 slice.24
  45.0 0.1 reshape.140
  45.1 0.7 reshape.142.place_ref
  45.9 0.1 broadcast_in_dim_reshape.4
  45.9 0.4 fusion
  46.3 4.2 %sort.7.keys_ref = s32[768]{0:T(1024)} sort(s32[768]{0:T(1024)S(1)} %get-tuple-element.11), dimensions={0}, to_apply=%region_2.3 | sort | flops 7680 | bytes 6144 | tf_op jit(solution)/shard_map/sort | solution.py:376
  50.6 0.1 gt.12
  50.6 0.7 convert_reduce_fusion
  51.4 30.4 %facet.1 = (f32[2,512,256]{2,1,0:T(8,128)}, f32[2,512,256]{2,1,0:T(8,128)}) custom-call(s32[1]{0:T(128)} %bitcast.5.count_ref, s32[768]{0:T(1024)} %sort.7.keys_ref, s32[3072]{0:T(1024)} %reshape.142.place_ref, s32[1]{0:T(128)} %bitcast.7.vis_ref, f32[784,8,128]{2,1,0:T(8,128)} %gather.7.block_ref, f32[8,64,128]{2,1,0:T(8,128)} %get-tuple-element.18.screen_a_ref, ...), custom_call_target="tpu_custom_call" | custom-call | tf_op jit(solution)/shard_map/facet/pallas_call | solution.py:388
  81.7 3.5 %collective-permute-start.1 = (f32[2,512,256]{2,1,0:T(8,128)}, f32[2,512,256]{2,1,0:T(8,128)S(1)}, u32[]{:S(2)}, u32[]{:S(2)}) collective-permute-start(f32[2,512,256]{2,1,0:T(8,128)} %get-tuple-element.8), channel_id=1, source_target_pairs={{0,1},{1,0},{2,3},{3,2},{4,5},{5,4},{6,7},{7,6},{8,9},{9,8},{10,11... | collective-permute-start | bytes 3145736 | tf_op jit(solution)/shard_map/ppermute | solution.py:401
  85.2 2.5 %collective-permute-done.1 = f32[2,512,256]{2,1,0:T(8,128)S(1)} collective-permute-done((f32[2,512,256]{2,1,0:T(8,128)}, f32[2,512,256]{2,1,0:T(8,128)S(1)}, u32[]{:S(2)}, u32[]{:S(2)}) %collective-permute-start.1) | collective-permute-done | bytes 1048608 | tf_op jit(solution)/shard_map/ppermute | solution.py:401
  87.7 2.3 %add.63 = f32[2,512,256]{2,1,0:T(8,128)} add(f32[2,512,256]{2,1,0:T(8,128)} %get-tuple-element.7, f32[2,512,256]{2,1,0:T(8,128)S(1)} %collective-permute-done.1) | non-fusion elementwise | flops 262144 | bytes 3145728 | tf_op jit(solution)/shard_map/add | solution.py:401
  (15 shorter events, 0.2 us)
Async XLA Ops:
  0.0 3.7 %copy-start = (f32[130816]{0:T(1024)S(1)}, f32[130816]{0:T(1024)}, u32[]{:S(2)}) copy-start(f32[130816]{0:T(1024)} %param.17) | copy-start | bytes 1569796
  0.0 8.8 %copy-start.1 = (f32[96,2,256]{2,1,0:T(2,128)S(1)}, f32[96,2,256]{2,1,0:T(2,128)}, u32[]{:S(2)}) copy-start(f32[96,2,256]{2,1,0:T(2,128)} %param.12) | copy-start | bytes 589828
  2.2 7.0 %collective-permute-start = (f32[1,8,128]{2,1,0:T(8,128)S(1)}, f32[1,8,128]{2,1,0:T(8,128)S(1)}, u32[]{:S(2)}, u32[]{:S(2)}) collective-permute-start(f32[1,8,128]{2,1,0:T(8,128)S(1)} %pad_bitcast_fusion), channel_id=1, source_target_pairs={{0,1},{1,0},{2,3},{3,2},{4,5},{5,4},{6,7},{7,6},{8,9},{9,8},{10,11... | collective-permute-start | bytes 12296 | tf_op jit(solution)/shard_map/ppermute | solution.py:352
  81.7 6.0 %collective-permute-start.1 = (f32[2,512,256]{2,1,0:T(8,128)}, f32[2,512,256]{2,1,0:T(8,128)S(1)}, u32[]{:S(2)}, u32[]{:S(2)}) collective-permute-start(f32[2,512,256]{2,1,0:T(8,128)} %get-tuple-element.8), channel_id=1, source_target_pairs={{0,1},{1,0},{2,3},{3,2},{4,5},{5,4},{6,7},{7,6},{8,9},{9,8},{10,11... | collective-permute-start | bytes 3145736 | tf_op jit(solution)/shard_map/ppermute | solution.py:401
